TPU v7x, 32 devices: a whole 2x2x4 slice. The times are simulated.
32 devices in a mesh: clip: 4 (over y, core), frame: 8 (over z, x).
Axes of the slice: x: 2, y: 2, z: 4, core: 2. Of those that a mesh axis runs over, the one named last changes fastest.
Arguments:
- x_in: bfloat16 [64, 20, 20, 1024], P(('clip', 'frame')), may hold values from -8 to 8
- cotangent: bfloat16 [64, 20, 20, 1024], P(('clip', 'frame')), may hold values from -6 to 6
- w_reduce: bfloat16 [1024, 256], P('frame'), may hold values from -0.1875 to 0.1875
- w_spatial: bfloat16 [3, 3, 256, 256], P(None, None, 'frame'), may hold values from -0.125 to 0.125
- w_expand: bfloat16 [256, 1024], P('frame'), may hold values from -0.375 to 0.375
- gain_one: bfloat16 [256], P('frame'), may hold values from 0.5 to 1.5
- shift_one: bfloat16 [256], P('frame'), may hold values from -2 to 2
- gain_two: bfloat16 [256], P('frame'), may hold values from 0.5 to 1.5
- shift_two: bfloat16 [256], P('frame'), may hold values from -2 to 2
- gain_three: bfloat16 [1024], P('frame'), may hold values from 0.5 to 1.5
- shift_three: bfloat16 [1024], P('frame'), may hold values from -2 to 2
- bucket: int32 [64], P(('clip', 'frame')), may hold values from 0 to 1
- frame_count: int32 [32], P(('clip', 'frame')), may hold values from 1 to 2, as said below
Outputs:
- output: bfloat16 [64, 20, 20, 1024], P(('clip', 'frame'))
- grad_in: bfloat16 [64, 20, 20, 1024], P(('clip', 'frame'))
- grad_reduce: float32 [1024, 256], P('frame')
- grad_spatial: float32 [3, 3, 256, 256], P(None, None, 'frame')
- grad_expand: float32 [256, 1024], P('frame')
- grad_gain_one: float32 [256], P('frame')
- grad_shift_one: float32 [256], P('frame')
- grad_gain_two: float32 [256], P('frame')
- grad_shift_two: float32 [256], P('frame')
- grad_gain_three: float32 [1024], P('frame')
- grad_shift_three: float32 [1024], P('frame')
Inputs may be any that keep to these rules, and one draw needn't show every extreme that they name: A device's used frames fill its first frame_count slots; in every draw some device uses all 2 slots.
All inputs are finite; a program needn't handle non-finite values.
Results may differ from a plain program's by a relative error of at most 0.017.
Values may be sent and summed in bfloat16 or wider, within the bound.
A program may use at most 64 MiB of HBM per device.

v0:
```python
import jax
import jax.numpy as jnp
from jax import lax
from jax.sharding import PartitionSpec as P

FRAME_SIDE = 20
SMALL_SIDE = 14


eps_norm = 1e-05


def silu_slope(values):
    sigma = jax.nn.sigmoid(values)
    return sigma * (1.0 + values * (1.0 - sigma))


def spatial_forward(inputs, kernel):
    side = inputs.shape[1]
    padded = jnp.pad(inputs, ((0, 0), (1, 1), (1, 1), (0, 0)))
    result = jnp.zeros(inputs.shape[:3] + (kernel.shape[3],), jnp.float32)
    for row_off in range(3):
        for col_off in range(3):
            window = padded[:, row_off : row_off + side, col_off : col_off + side]
            result = result + jnp.einsum(
                "fhwc,cd->fhwd",
                window,
                kernel[row_off, col_off],
                preferred_element_type=jnp.float32,
            )
    return result


def spatial_backward(inputs, grad_out, kernel):
    side = inputs.shape[1]
    padded = jnp.pad(inputs, ((0, 0), (1, 1), (1, 1), (0, 0)))
    kernel_rows = []
    grad_padded = jnp.zeros(padded.shape, jnp.float32)
    for row_off in range(3):
        kernel_cols = []
        for col_off in range(3):
            window = padded[:, row_off : row_off + side, col_off : col_off + side]
            kernel_cols.append(
                jnp.einsum("fhwc,fhwd->cd", window, grad_out, preferred_element_type=jnp.float32)
            )
            term = jnp.einsum(
                "fhwd,cd->fhwc",
                grad_out,
                kernel[row_off, col_off],
                preferred_element_type=jnp.float32,
            )
            grad_padded = grad_padded + jnp.pad(
                term, ((0, 0), (row_off, 2 - row_off), (col_off, 2 - col_off), (0, 0))
            )
        kernel_rows.append(jnp.stack(kernel_cols))
    return (jnp.stack(kernel_rows), grad_padded[:, 1:-1, 1:-1])


def on_device(
    x_in,
    cotangent,
    w_reduce,
    w_spatial,
    w_expand,
    gain_one,
    shift_one,
    gain_two,
    shift_two,
    gain_three,
    shift_three,
    bucket,
    frame_count,
):
    frames = x_in.shape[0]
    side = x_in.shape[1]
    slots = jnp.arange(frames, dtype=jnp.int32)
    live = slots < frame_count[0]
    extent = jnp.where(bucket == 0, SMALL_SIDE, FRAME_SIDE)
    places = jnp.arange(side, dtype=jnp.int32)
    inside = (
        (places[None, :, None] < extent[:, None, None])
        & (places[None, None, :] < extent[:, None, None])
        & live[:, None, None]
    )
    pixel_mask = inside.astype(jnp.float32)[..., None]
    local_count = jnp.sum(pixel_mask)

    def normalize(values, gain, shift):
        total, squares, count = lax.psum(
            (
                jnp.sum(values * pixel_mask, axis=(0, 1, 2)),
                jnp.sum(values * values * pixel_mask, axis=(0, 1, 2)),
                local_count,
            ),
            ("clip", "frame"),
        )
        mean = total / count
        var = squares / count - mean * mean
        inv_std = lax.rsqrt(var + eps_norm)
        scaled = (values - mean) * inv_std
        return (
            scaled,
            inv_std,
            count,
            scaled * gain.astype(jnp.float32) + shift.astype(jnp.float32),
        )

    def norm_back(grad_z, scaled, inv_std, gain, count):
        shift_grad, gain_grad = lax.psum(
            (jnp.sum(grad_z, axis=(0, 1, 2)), jnp.sum(grad_z * scaled, axis=(0, 1, 2))),
            ("clip", "frame"),
        )
        grad_pre = (
            pixel_mask
            * inv_std
            * gain.astype(jnp.float32)
            * (grad_z - shift_grad / count - scaled * gain_grad / count)
        )
        return (grad_pre.astype(jnp.bfloat16), gain_grad, shift_grad)

    local_params = (
        w_reduce,
        w_spatial,
        w_expand,
        gain_one,
        shift_one,
        gain_two,
        shift_two,
        gain_three,
        shift_three,
    )
    gathered = (
        lax.all_gather(local_params[0], "frame", axis=0, tiled=True),
        lax.all_gather(local_params[1], "frame", axis=2, tiled=True),
        lax.all_gather(local_params[2], "frame", axis=0, tiled=True),
        lax.all_gather(local_params[3], "frame", axis=0, tiled=True),
        lax.all_gather(local_params[4], "frame", axis=0, tiled=True),
        lax.all_gather(local_params[5], "frame", axis=0, tiled=True),
        lax.all_gather(local_params[6], "frame", axis=0, tiled=True),
        lax.all_gather(local_params[7], "frame", axis=0, tiled=True),
        lax.all_gather(local_params[8], "frame", axis=0, tiled=True),
    )
    full_reduce, full_spatial, full_expand, full_g1, full_b1, full_g2, full_b2, full_g3, full_b3 = (
        gathered
    )
    masked_in = (x_in.astype(jnp.float32) * pixel_mask).astype(jnp.bfloat16)
    pre_one = jnp.einsum(
        "fhwc,cd->fhwd", masked_in, full_reduce, preferred_element_type=jnp.float32
    )
    scaled_one, inv_one, count, z_one = normalize(pre_one, full_g1, full_b1)
    act_one = (pixel_mask * jax.nn.silu(z_one)).astype(jnp.bfloat16)
    pre_two = spatial_forward(act_one, full_spatial)
    scaled_two, inv_two, count, z_two = normalize(pre_two, full_g2, full_b2)
    act_two = (pixel_mask * jax.nn.silu(z_two)).astype(jnp.bfloat16)
    pre_three = jnp.einsum(
        "fhwd,dc->fhwc", act_two, full_expand, preferred_element_type=jnp.float32
    )
    scaled_three, inv_three, count, z_three = normalize(pre_three, full_g3, full_b3)
    total = z_three + masked_in.astype(jnp.float32)
    output = (pixel_mask * jax.nn.silu(total)).astype(jnp.bfloat16)
    again_params = (
        lax.all_gather(local_params[0], "frame", axis=0, tiled=True),
        lax.all_gather(local_params[1], "frame", axis=2, tiled=True),
        lax.all_gather(local_params[2], "frame", axis=0, tiled=True),
        lax.all_gather(local_params[3], "frame", axis=0, tiled=True),
        lax.all_gather(local_params[4], "frame", axis=0, tiled=True),
        lax.all_gather(local_params[5], "frame", axis=0, tiled=True),
        lax.all_gather(local_params[6], "frame", axis=0, tiled=True),
        lax.all_gather(local_params[7], "frame", axis=0, tiled=True),
        lax.all_gather(local_params[8], "frame", axis=0, tiled=True),
    )
    (
        back_reduce,
        back_spatial,
        back_expand,
        back_g1,
        unused_one,
        back_g2,
        unused_two,
        back_g3,
        unused_three,
    ) = again_params
    grad_total = pixel_mask * cotangent.astype(jnp.float32) * silu_slope(total)
    grad_pre_three, grad_gain_three, grad_shift_three = norm_back(
        grad_total, scaled_three, inv_three, back_g3, count
    )
    grad_expand = jnp.einsum(
        "fhwd,fhwc->dc", act_two, grad_pre_three, preferred_element_type=jnp.float32
    )
    grad_act_two = jnp.einsum(
        "fhwc,dc->fhwd", grad_pre_three, back_expand, preferred_element_type=jnp.float32
    )
    dz_two = pixel_mask * grad_act_two * silu_slope(z_two)
    grad_pre_two, grad_gain_two, grad_shift_two = norm_back(
        dz_two, scaled_two, inv_two, back_g2, count
    )
    grad_spatial, grad_act_one = spatial_backward(act_one, grad_pre_two, back_spatial)
    dz_one = pixel_mask * grad_act_one * silu_slope(z_one)
    grad_pre_one, grad_gain_one, grad_shift_one = norm_back(
        dz_one, scaled_one, inv_one, back_g1, count
    )
    grad_reduce = jnp.einsum(
        "fhwc,fhwd->cd", masked_in, grad_pre_one, preferred_element_type=jnp.float32
    )
    back_input = jnp.einsum(
        "fhwd,cd->fhwc", grad_pre_one, back_reduce, preferred_element_type=jnp.float32
    )
    grad_in = (pixel_mask * (back_input + grad_total)).astype(jnp.bfloat16)
    owned = (
        lax.psum_scatter(
            grad_reduce.astype(jnp.bfloat16), "frame", scatter_dimension=0, tiled=True
        ).astype(jnp.float32),
        lax.psum_scatter(
            grad_spatial.astype(jnp.bfloat16), "frame", scatter_dimension=2, tiled=True
        ).astype(jnp.float32),
        lax.psum_scatter(
            grad_expand.astype(jnp.bfloat16), "frame", scatter_dimension=0, tiled=True
        ).astype(jnp.float32),
    )
    shard_reduce, shard_spatial, shard_expand = (
        lax.psum(owned[0].astype(jnp.bfloat16), "clip").astype(jnp.float32),
        lax.psum(owned[1].astype(jnp.bfloat16), "clip").astype(jnp.float32),
        lax.psum(owned[2].astype(jnp.bfloat16), "clip").astype(jnp.float32),
    )
    position = lax.axis_index("frame")
    narrow_part = gain_one.shape[0]
    broad_part = gain_three.shape[0]

    def own_slice(values, width):
        return lax.dynamic_slice_in_dim(values, position * width, width)

    return (
        output,
        grad_in,
        shard_reduce,
        shard_spatial,
        shard_expand,
        own_slice(grad_gain_one, narrow_part),
        own_slice(grad_shift_one, narrow_part),
        own_slice(grad_gain_two, narrow_part),
        own_slice(grad_shift_two, narrow_part),
        own_slice(grad_gain_three, broad_part),
        own_slice(grad_shift_three, broad_part),
    )


def solution(mesh):
    return jax.shard_map(
        on_device,
        mesh=mesh,
        in_specs=(
            P(("clip", "frame"), None, None, None),
            P(("clip", "frame"), None, None, None),
            P("frame", None),
            P(None, None, "frame", None),
            P("frame", None),
            P("frame"),
            P("frame"),
            P("frame"),
            P("frame"),
            P("frame"),
            P("frame"),
            P(("clip", "frame")),
            P(("clip", "frame")),
        ),
        out_specs=(
            P(("clip", "frame"), None, None, None),
            P(("clip", "frame"), None, None, None),
            P("frame", None),
            P(None, None, "frame", None),
            P("frame", None),
            P("frame"),
            P("frame"),
            P("frame"),
            P("frame"),
            P("frame"),
            P("frame"),
        ),
        check_vma=False,
    )
```

profile of v0, /device:TPU:0, one launch (start us, length us, event | category | flops | bytes accessed | tf_op | source)
XLA Modules:
  0.0 619.4 jit_solution(12198950948304453179)
XLA Ops:
  7.2 0.7 all-gather.4.cloned.1.call-update
  8.0 0.7 compare_select_fusion
  9.5 1.2 dynamic-slice
  11.4 0.9 dynamic-update-slice
  12.2 0.8 dynamic-update-slice.1
  13.1 0.8 dynamic-update-slice.2
  13.9 0.8 dynamic-update-slice.3
  14.8 23.2 %all-reduce.20 = (bf16[256]{0:T(256)(128)(2,1)S(1)}, bf16[256]{0:T(256)(128)(2,1)S(1)}, bf16[256]{0:T(256)(128)(2,1)S(1)}, bf16[256]{0:T(256)(128)(2,1)S(1)}) all-reduce(bf16[256]{0:T(256)(128)(2,1)S(1)} %dynamic-update-slice.1, bf16[256]{0:T(256)(128)(2,1)S(1)} %dynamic-update-slice, ...), channel_id=1, replica_groups=mesh['clip'=4,'frame'=8] {'frame'}, use_global_device_ids=true, to_apply=%add.11 | all-reduce | flops 1024 | bytes 4096
  38.0 16.4 %all-gather = bf16[8,1,128]{2,1,0:T(2,128)(2,1)S(1)} all-gather(bf16[1,1,128]{2,1,0:T(2,128)(2,1)} %bitcast.236), channel_id=1, replica_groups=mesh['clip'=4,'frame'=8] {'frame'}, dimensions={0}, use_global_device_ids=true | all-gather | bytes 2304 | tf_op jit(solution)/shard_map/all_gather | solution.py:140
  54.4 18.2 %all-gather.1 = bf16[8,1,128]{2,1,0:T(2,128)(2,1)S(1)} all-gather(bf16[1,1,128]{2,1,0:T(2,128)(2,1)} %bitcast.237), channel_id=1, replica_groups=mesh['clip'=4,'frame'=8] {'frame'}, dimensions={0}, use_global_device_ids=true | all-gather | bytes 2304 | tf_op jit(solution)/shard_map/all_gather | solution.py:141
  72.7 0.7 fusion.55
  73.4 31.6 %all_gather.33 = bf16[1024,256]{1,0:T(8,128)(2,1)S(1)} all-gather(bf16[128,256]{1,0:T(8,128)(2,1)} %param.15), channel_id=1, replica_groups=mesh['clip'=4,'frame'=8] {'frame'}, dimensions={0}, use_global_device_ids=true | all-gather | bytes 589824 | tf_op jit(solution)/shard_map/all_gather | solution.py:133
  105.0 2.7 multiply_reduce_fusion.7
  107.7 37.2 %all-reduce.19 = (f32[256]{0:T(256)S(1)}, f32[]{:T(128)}, f32[256]{0:T(256)S(1)}) all-reduce(f32[256]{0:T(256)S(1)} %get-tuple-element.51, f32[]{:T(128)} %fusion.55, f32[256]{0:T(256)S(1)} %get-tuple-element.50), channel_id=1, replica_groups=mesh['clip'=4,'frame'=8] {'clip','frame'}, use_global_device_ids=true, to_apply=%region_1.2 | all-reduce | flops 513 | bytes 4104 | tf_op jit(solution)/shard_map/psum | solution.py:89
  144.9 0.7 add_rsqrt_fusion.2
  145.6 33.5 %all_gather.39 = bf16[256,1024]{1,0:T(8,128)(2,1)} all-gather(bf16[32,1024]{1,0:T(8,128)(2,1)S(1)} %copy-done.13), channel_id=1, replica_groups=mesh['clip'=4,'frame'=8] {'frame'}, dimensions={0}, use_global_device_ids=true | all-gather | bytes 589824 | tf_op jit(solution)/shard_map/all_gather | solution.py:135
  179.1 0.4 multiply_convert_fusion.9
  179.5 1.3 fusion.44
  180.8 1.2 convolution_add_fusion.7
  184.0 1.3 multiply_reduce_fusion.5
  185.3 39.5 %all-reduce.18 = (f32[256]{0:T(256)S(1)}, f32[256]{0:T(256)S(1)}) all-reduce(f32[256]{0:T(256)S(1)} %get-tuple-element.49, f32[256]{0:T(256)S(1)} %get-tuple-element.48), channel_id=1, replica_groups=mesh['clip'=4,'frame'=8] {'clip','frame'}, use_global_device_ids=true, to_apply=%region_7.8 | all-reduce | flops 512 | bytes 4096 | tf_op jit(solution)/shard_map/psum | solution.py:89
  224.8 0.7 add_rsqrt_fusion.1
  225.5 4.3 multiply_reduce_fusion.2
  229.8 40.5 %all-reduce.17 = (f32[1024]{0:T(1024)S(1)}, f32[1024]{0:T(1024)S(1)}) all-reduce(f32[1024]{0:T(1024)S(1)} %get-tuple-element.45, f32[1024]{0:T(1024)S(1)} %get-tuple-element.44), channel_id=1, replica_groups=mesh['clip'=4,'frame'=8] {'clip','frame'}, use_global_device_ids=true, to_apply=%region_13.14 | all-reduce | flops 2048 | bytes 16384 | tf_op jit(solution)/shard_map/psum | solution.py:89
  270.3 0.7 broadcast_divide_fusion.1
  271.0 7.1 %fusion.72 = (f32[1024]{0:T(1024)S(1)}, f32[1024]{0:T(1024)S(1)}, f32[2,20,20,1024]{3,2,1,0:T(8,128)}, bf16[2,20,20,1024]{3,2,1,0:T(8,128)(2,1)}) fusion(f32[1024]{0:T(1024)S(1)} %get-tuple-element.84, f32[2,20,20,1024]{3,2,1,0:T(8,128)} %get-tuple-element.87, f32[1024]{0:T(1024)S(1)} %get-tuple-element.83, bf16[2,20,20,1024]{3,0,2,1:T(2,128)(2,1)} %param.13, ...), kind=kLoop, calls=%fused_computation.155 | loop fusion | flops 20477952 | bytes 11496576 | tf_op jit(solution)/shard_map/reduce_sum | solution.py:110
  278.0 39.8 %all-reduce.16 = (f32[1024]{0:T(1024)S(1)}, f32[1024]{0:T(1024)S(1)}) all-reduce(f32[1024]{0:T(1024)S(1)} %get-tuple-element.47, f32[1024]{0:T(1024)S(1)} %get-tuple-element.46), channel_id=1, replica_groups=mesh['clip'=4,'frame'=8] {'clip','frame'}, use_global_device_ids=true, to_apply=%region_17.18 | all-reduce | flops 2048 | bytes 16384 | tf_op jit(solution)/shard_map/psum | solution.py:109
  317.8 0.6 broadcast_divide_fusion
  318.5 5.3 multiply_convert_fusion.1
  323.8 1.3 copy-done.5
  325.1 1.7 fusion.2
  326.8 4.0 fusion.74
  330.8 40.6 %all-reduce.15 = (f32[256]{0:T(256)S(1)}, f32[256]{0:T(256)S(1)}) all-reduce(f32[256]{0:T(256)S(1)} %get-tuple-element.55, f32[256]{0:T(256)S(1)} %get-tuple-element.54), channel_id=1, replica_groups=mesh['clip'=4,'frame'=8] {'clip','frame'}, use_global_device_ids=true, to_apply=%region_21.22 | all-reduce | flops 512 | bytes 4096 | tf_op jit(solution)/shard_map/psum | solution.py:109
  371.3 0.6 broadcast_divide_fusion.3
  372.0 2.5 multiply_convert_fusion.7
  374.5 0.4 fusion.15
  375.2 1.0 fusion.18
  376.2 1.0 fusion.12
  377.2 1.0 fusion.13
  378.2 1.0 fusion.14
  382.6 1.3 fusion.73
  383.8 39.5 %all-reduce.14 = (f32[256]{0:T(256)S(1)}, f32[256]{0:T(256)S(1)}) all-reduce(f32[256]{0:T(256)S(1)} %get-tuple-element.53, f32[256]{0:T(256)S(1)} %get-tuple-element.52), channel_id=1, replica_groups=mesh['clip'=4,'frame'=8] {'clip','frame'}, use_global_device_ids=true, to_apply=%region_25.26 | all-reduce | flops 512 | bytes 4096 | tf_op jit(solution)/shard_map/psum | solution.py:109
  423.3 0.8 broadcast_divide_fusion.2
  424.1 1.0 multiply_convert_fusion.6
  425.1 0.8 copy-done.6
  425.9 1.9 fusion.1
  429.2 0.6 copy-done.9
  429.9 1.1 pad_maximum_fusion
  431.1 10.9 %reduce-scatter.8.cloned.1.call-done = bf16[32,1024]{1,0:T(8,128)(2,1)} async-done(((bf16[256,1024]{1,0:T(8,128)(2,1)}), bf16[32,1024]{1,0:T(8,128)(2,1)}) %reduce-scatter.8.cloned.1.call-update) | async-done | bytes 65552 | tf_op jit(solution)/shard_map/reduce_scatter | solution.py:216
  442.0 65.2 %reduce-scatter.4.cloned.1.call-done = bf16[128,256]{1,0:T(8,128)(2,1)} async-done(((bf16[1024,256]{1,0:T(8,128)(2,1)}), bf16[128,256]{1,0:T(8,128)(2,1)}) %reduce-scatter.4.cloned.1.call-update) | async-done | bytes 65552 | tf_op jit(solution)/shard_map/reduce_scatter | solution.py:210
  507.2 67.5 %reduce-scatter.6.cloned.1.call-done = bf16[3,3,32,256]{3,2,1,0:T(8,128)(2,1)} async-done(((bf16[3,3,256,256]{3,2,1,0:T(8,128)(2,1)}), bf16[3,3,32,256]{3,2,1,0:T(8,128)(2,1)}) %reduce-scatter.6.cloned.1.call-update) | async-done | bytes 147472 | tf_op jit(solution)/shard_map/reduce_scatter | solution.py:213
  574.8 2.8 multiply_convert_fusion
  577.7 0.6 dynamic_slice.18
  578.2 0.6 dynamic_slice.19
  578.8 0.6 dynamic_slice.20
  579.4 0.6 dynamic_slice.21
  580.0 0.6 dynamic_slice.22
  580.6 0.6 dynamic_slice.23
  581.2 2.9 copy.36
  584.0 2.9 copy.35
  586.9 21.4 %all-reduce.24.cloned.1.call-done = (bf16[128,256]{1,0:T(8,128)(2,1)}, bf16[3,3,32,256]{3,2,1,0:T(8,128)(2,1)}, bf16[32,1024]{1,0:T(8,128)(2,1)}) async-done(((bf16[128,256]{1,0:T(8,128)(2,1)}, bf16[3,3,32,256]{3,2,1,0:T(8,128)(2,1)}, bf16[32,1024]{1,0:T(8,128)(2,1)}), (bf16[128,256]{1,0:T(8,128)(2,1)}, bf16[3,3,32,256]{3,2,1,0:T(8,128)(2,1)}, bf16[32,1024]{1,0:T(8,128)(2,1)})) %all-reduce.24.cloned.1.call-update) | async-done | bytes 278544 | tf_op jit(solution)/shard_map/psum | solution.py:221
  608.2 1.6 convert_element_type.131
  609.9 1.5 convert_element_type.130
  611.4 1.5 convert_element_type.133
  (71 shorter events, 7.6 us)
Async XLA Ops:
  7.2 172.3 %all-gather.4.cloned.1.call-start = ((), (), s32[]{:S(2)}) async-start(), calls=%async_computation.3 | async-start | bytes 1327104 | tf_op jit(solution)/shard_map/all_gather | solution.py:134
  7.9 434.1 %reduce-scatter.8.cloned.1.call-start = ((), (), s32[]{:S(2)}) async-start(), calls=%async_computation.6 | async-start | bytes 589824 | tf_op jit(solution)/shard_map/reduce_scatter | solution.py:216
  105.0 2.7 copy-start.3
  105.0 40.5 %copy-start.13 = (bf16[32,1024]{1,0:T(8,128)(2,1)S(1)}, bf16[32,1024]{1,0:T(8,128)(2,1)}, u32[]{:S(2)}) copy-start(bf16[32,1024]{1,0:T(8,128)(2,1)} %param.17) | copy-start | bytes 196612
  179.5 2.5 copy-start.1
  318.4 6.6 %copy-start.2 = (f32[2,20,20,256]{3,2,1,0:T(8,128)S(1)}, f32[2,20,20,256]{3,2,1,0:T(8,128)}, u32[]{:S(2)}) copy-start(f32[2,20,20,256]{3,2,1,0:T(8,128)} %get-tuple-element.86) | copy-start | bytes 2457604
  323.8 1.3 copy-start.5
  379.3 128.0 %reduce-scatter.4.cloned.1.call-start = ((), (), s32[]{:S(2)}) async-start(), calls=%async_computation.4 | async-start | bytes 589824 | tf_op jit(solution)/shard_map/reduce_scatter | solution.py:210
  423.3 2.6 copy-start.8
  425.1 0.8 copy-start.6
  425.9 2.2 copy-start.10
  425.9 2.2 copy-start.11
  425.9 2.2 copy-start.12
  427.8 147.0 %reduce-scatter.6.cloned.1.call-start = ((), (), s32[]{:S(2)}) async-start(), calls=%async_computation.5 | async-start | bytes 1327104 | tf_op jit(solution)/shard_map/reduce_scatter | solution.py:213
  428.9 0.9 copy-start.9
  429.9 144.9 %copy-start.4 = (bf16[1024,256]{1,0:T(8,128)(2,1)S(1)}, bf16[1024,256]{1,0:T(8,128)(2,1)}, u32[]{:S(2)}) copy-start(bf16[1024,256]{1,0:T(8,128)(2,1)} %copy-done.3) | copy-start | bytes 1572868
  429.9 144.9 %copy-start.7 = (bf16[2,20,20,256]{3,2,1,0:T(8,128)(2,1)S(1)}, bf16[2,20,20,256]{3,2,1,0:T(8,128)(2,1)}, u32[]{:S(2)}) copy-start(bf16[2,20,20,256]{3,2,1,0:T(8,128)(2,1)} %copy-done.6) | copy-start | bytes 1228804
  431.1 177.2 %all-reduce.24.cloned.1.call-start = ((), (), s32[]{:S(2)}) async-start(), calls=%async_computation.7 | async-start | bytes 557056 | tf_op jit(solution)/shard_map/psum | solution.py:221
  577.6 6.4 %copy-start = (bf16[2,20,20,1024]{3,2,1,0:T(8,128)(2,1)S(1)}, bf16[2,20,20,1024]{3,2,1,0:T(8,128)(2,1)}, u32[]{:S(2)}) copy-start(bf16[2,20,20,1024]{3,2,1,0:T(8,128)(2,1)} %get-tuple-element.82) | copy-start | bytes 4915204
Sparse Core Ops, SparseCore 0:
  10.2 43.8 all-gather.3
  379.4 62.5 reduce-scatter.7
  446.3 60.8 reduce-scatter.3
  511.1 63.6 reduce-scatter.5
  577.1 31.0 all-reduce.23
where the time goes:
time: 621 us; the launch traced here: 619 us
  blocking collectives  360 us (58%)
  waiting for transfers between devices  166 us (27%)
  matrix products  31.9 us (5%)
  other arithmetic  29.2 us (5%)
  local copies, waits for them, and re-layouts  16.6 us (3%)
  between operations  15.5 us (2%)
    psum x3, blocking collectives, norm_back(): lax.psum((jnp.sum(grad_z, axis=(0, 1, 2)), jnp.sum(grad_z * scaled, axis=...  120 us
    psum x3, blocking collectives, normalize(): lax.psum((jnp.sum(values * pixel_mask, axis=(0, 1, 2)), jnp.sum(values *...  117 us
    reduce_scatter x1, waiting for transfers between devices, on_device(): lax.psum_scatter(grad_spatial.astype(jnp.bfloat16), 'frame', scatter_dime...  67.5 us
    reduce_scatter x1, waiting for transfers between devices, on_device(): lax.psum_scatter(grad_reduce.astype(jnp.bfloat16), 'frame', scatter_dimen...  65.2 us
    all_gather x1, blocking collectives, on_device(): lax.all_gather(local_params[2], 'frame', axis=0, tiled=True)  33.5 us
    all_gather x1, blocking collectives, on_device(): lax.all_gather(local_params[0], 'frame', axis=0, tiled=True)  31.6 us
    unnamed x1, blocking collectives  23.2 us
    psum x1, waiting for transfers between devices, on_device(): lax.psum(owned[0].astype(jnp.bfloat16), 'clip').astype(jnp.float32)  21.4 us
  transfers between devices with their start and end apart: 5, of which 4 were waited for; matrix products, arithmetic and copies ran while one was open for 5% of the time, Pallas kernels for 0%

commit v1 on v0

v1 whole, which is shorter than its diff:
```python
import functools

import jax
import jax.numpy as jnp
from jax import lax
from jax.experimental import pallas as pl
from jax.experimental.pallas import tpu as pltpu
from jax.sharding import PartitionSpec as P

SMALL_SIDE = 14
EPS = 1e-05
LANES = 128
BLOCK = 80
MESH = pl.DeviceIdType.MESH
F32 = jnp.float32
BF16 = jnp.bfloat16


def sigmoid(v):
    return 0.5 * jnp.tanh(0.5 * v) + 0.5


def part_sum(v):
    rows, width = v.shape
    return jnp.sum(v.reshape(rows // 8, 8, width), axis=0)


def dot(a, b):
    return jnp.dot(a, b, preferred_element_type=F32)


def dot_tn(a, b):
    return lax.dot_general(a, b, (((0,), (0,)), ((), ())), preferred_element_type=F32)


def rows_to_vec(tile, first, count):
    return jnp.concatenate([tile[first + i : first + i + 1] for i in range(count)], axis=1)


def block_kernel(
    dims,
    x_hbm,
    ct_hbm,
    wr_hbm,
    ws_hbm,
    we_hbm,
    g1_ref,
    b1_ref,
    g2_ref,
    b2_ref,
    g3_ref,
    b3_ref,
    bucket_ref,
    count_ref,
    out_hbm,
    gin_hbm,
    gr_out,
    gs_out,
    ge_out,
    vec1_gain,
    vec1_shift,
    vec2_gain,
    vec2_shift,
    vec3_gain,
    vec3_shift,
    xs,
    cs,
    os,
    xm,
    mask,
    left_ok,
    right_ok,
    wr,
    ws,
    we,
    wst,
    wet,
    wrt,
    pre1,
    slope1,
    pre2,
    slope2,
    dz,
    spad,
    act2,
    nine,
    pre3,
    gt,
    gp3,
    gp1,
    par,
    st1,
    st2,
    st3,
    st4,
    st5,
    st6,
    local_sem,
    wsend,
    wrecv,
    fsend,
    frecv,
    st_send,
    st_recv,
    out_sem,
    gr_ref,
    gs_ref,
    ge_ref,
    gr_core,
    gs_core,
    ge_core,
    gr_got,
    gs_got,
    ge_got,
    gr_fin,
    gs_fin,
    ge_fin,
    rs_send,
    rs_recv,
):
    clips, frames, side, own_gather = dims
    devices = clips * frames
    clip = lax.axis_index("clip")
    frame = lax.axis_index("frame")
    me = clip * frames + frame
    core = lax.rem(clip, 2)
    partner = (clip + 1 - 2 * core, frame)
    rows = xm.shape[0]
    channels = xm.shape[1]
    narrow = wr.shape[1]
    wide_tiles = channels // LANES
    nar_tiles = narrow // LANES
    blocks = rows // BLOCK
    pad = 2 * side

    def other(k):
        return (lax.rem(clip + lax.div(k, frames), clips), lax.rem(frame + lax.rem(k, frames), frames))

    for j in range(wide_tiles):
        lanes = pl.ds(LANES * j, LANES)
        pltpu.make_async_copy(x_hbm.at[:, :, lanes], xs.at[j], local_sem.at[0]).start()
    if own_gather:
        part_r = wr_hbm.shape[0]
        part_s = ws_hbm.shape[1]
        part_e = we_hbm.shape[0]
        own_r = wr.at[pl.ds(pl.multiple_of(frame * part_r, part_r), part_r)]
        own_s = ws.at[:, pl.ds(pl.multiple_of(frame * part_s, part_s), part_s)]
        own_e = we.at[pl.ds(pl.multiple_of(frame * part_e, part_e), part_e)]
    else:
        own_r, own_s, own_e = wr, ws, we
    own_copies = [
        pltpu.make_async_copy(wr_hbm, own_r, local_sem.at[2]),
        pltpu.make_async_copy(ws_hbm, own_s, local_sem.at[3]),
        pltpu.make_async_copy(we_hbm, own_e, local_sem.at[4]),
    ]
    for copy in own_copies:
        copy.start()
    for j in range(wide_tiles):
        lanes = pl.ds(LANES * j, LANES)
        pltpu.make_async_copy(ct_hbm.at[:, :, lanes], cs.at[j], local_sem.at[1]).start()

    barrier = pltpu.get_barrier_semaphore()

    def greet(k, carry):
        pl.semaphore_signal(barrier, inc=1, device_id=other(k), device_id_type=MESH)
        return carry

    lax.fori_loop(1, devices, greet, 0)

    row_id = lax.broadcasted_iota(jnp.int32, (rows, LANES), 0)
    pixel = row_id >> 1
    slot = row_id & 1
    line = (pixel * 3277) >> 16
    col = pixel - line * side
    extent = [jnp.where(bucket_ref[f] == 0, SMALL_SIDE, side) for f in range(2)]
    limit = [jnp.where(count_ref[0] > f, extent[f], 0) for f in range(2)]
    bound = jnp.where(slot == 0, limit[0], limit[1])
    live = ((line < bound) & (col < bound)).astype(F32)
    mask[...] = live
    left_ok[...] = (col >= 1).astype(F32)
    right_ok[...] = (col <= side - 2).astype(F32)

    tile = jnp.zeros((8, LANES), F32)
    par[me] = tile
    for i, ref in enumerate((g1_ref, b1_ref, g2_ref, b2_ref, g3_ref, b3_ref)):
        width = ref.shape[0]
        par[me, i : i + 1, 0:width] = ref[...].astype(F32).reshape(1, width)
    par[me, 6:7, :] = jnp.sum(live, axis=0, keepdims=True)

    pl.semaphore_wait(barrier, devices - 1)

    def gather_to_all(buf, index):
        def send(k, carry):
            pltpu.make_async_remote_copy(
                src_ref=buf.at[me],
                dst_ref=buf.at[me],
                send_sem=st_send.at[index],
                recv_sem=st_recv.at[index],
                device_id=other(k),
                device_id_type=MESH,
            ).start()
            return carry

        lax.fori_loop(1, devices, send, 0)

    def arrived(buf, index):
        most = buf.at[pl.ds(0, devices - 1)]
        pltpu.make_async_copy(most, most, st_recv.at[index]).wait()
        pltpu.make_async_copy(most, most, st_send.at[index]).wait()
        return jnp.sum(buf[...], axis=0)

    own_copies[0].wait()
    own_copies[1].wait()
    own_copies[2].wait()
    gather_to_all(par, 0)
    if own_gather:

        def halves(ref, axis, part):
            half = part // 2

            def view(owner):
                at = pl.ds(pl.multiple_of(owner * part + core * half, half), half)
                return ref.at[at] if axis == 0 else ref.at[:, at]

            return view

        views = (halves(wr, 0, part_r), halves(ws, 1, part_s), halves(we, 0, part_e))

        def weight_send(index):
            view = views[index]

            def send(b, carry):
                pltpu.make_async_remote_copy(
                    src_ref=view(frame),
                    dst_ref=view(frame),
                    send_sem=wsend.at[index, b],
                    recv_sem=wrecv.at[index, b],
                    device_id=(clip, lax.rem(frame + b, frames)),
                    device_id_type=MESH,
                ).start()
                return carry

            lax.fori_loop(1, frames, send, 0)

        def weight_pass(index):
            view = views[index]

            def step(b, carry):
                owner = lax.rem(frame - b + frames, frames)
                pltpu.make_async_remote_copy(
                    src_ref=view(owner),
                    dst_ref=view(owner),
                    send_sem=wsend.at[index, b],
                    recv_sem=wrecv.at[index, b],
                    device_id=partner,
                    device_id_type=MESH,
                ).wait()
                pltpu.make_async_remote_copy(
                    src_ref=view(owner),
                    dst_ref=view(owner),
                    send_sem=fsend.at[index, b],
                    recv_sem=frecv.at[index, b],
                    device_id=partner,
                    device_id_type=MESH,
                ).start()
                return carry

            lax.fori_loop(1, frames, step, 0)

        def weight_wait(index):
            view = views[index]

            def step(b, carry):
                owner = lax.rem(frame - b + frames, frames)
                pltpu.make_async_remote_copy(
                    src_ref=view(owner),
                    dst_ref=view(owner),
                    send_sem=fsend.at[index, b],
                    recv_sem=frecv.at[index, b],
                    device_id=partner,
                    device_id_type=MESH,
                ).wait()
                return carry

            lax.fori_loop(1, frames, step, 0)

        for index in range(3):
            weight_send(index)
    else:

        def weight_pass(index):
            pass

        def weight_wait(index):
            pass

    pltpu.make_async_copy(xs, xs, local_sem.at[0]).wait()
    xs_rows = xs.reshape(wide_tiles, rows, LANES)
    cs_rows = cs.reshape(wide_tiles, rows, LANES)
    os_rows = os.reshape(wide_tiles, rows, LANES)

    def block_at(i):
        return pl.ds(pl.multiple_of(i * BLOCK, BLOCK), BLOCK)

    def mask_in(i, carry):
        at = block_at(i)
        m = mask[at, :].astype(BF16)
        for j in range(wide_tiles):
            xm[at, LANES * j : LANES * (j + 1)] = xs_rows[j, at, :] * m
        return carry

    lax.fori_loop(0, blocks, mask_in, 0)
    edge = jnp.zeros((3, pad, narrow), F32)
    spad[:, 0:pad, :] = edge
    spad[:, pad + rows : 2 * pad + rows, :] = edge

    weight_pass(0)
    weight_wait(0)

    all_par = arrived(par, 0)
    count = all_par[6:7, :]
    part_n = g1_ref.shape[0]
    part_w = g3_ref.shape[0]
    acc_n = [jnp.zeros((8, LANES), F32) for _ in range(nar_tiles)]
    acc_w = [jnp.zeros((8, LANES), F32) for _ in range(wide_tiles)]
    for f in range(frames):
        tile = par[f]
        spot = f * part_n
        shift = spot % LANES
        acc_n[spot // LANES] += pltpu.roll(tile, shift, 1) if shift else tile
        spot = f * part_w
        shift = spot % LANES
        acc_w[spot // LANES] += pltpu.roll(tile, shift, 1) if shift else tile
    gain1, bias1, gain2, bias2 = [jnp.concatenate([a[i : i + 1] for a in acc_n], axis=1) for i in range(4)]
    gain3, bias3 = [jnp.concatenate([a[i : i + 1] for a in acc_w], axis=1) for i in (4, 5)]
    inv_count = 1.0 / count
    inv_n = jnp.concatenate([inv_count] * nar_tiles, axis=1)
    inv_w = jnp.concatenate([inv_count] * wide_tiles, axis=1)

    def send_sums(buf, index, first, second):
        tiles = first.shape[1] // LANES
        first = jnp.sum(first, axis=0, keepdims=True)
        second = jnp.sum(second, axis=0, keepdims=True)
        for i in range(tiles):
            buf[me, i : i + 1, :] = first[:, LANES * i : LANES * (i + 1)]
            buf[me, tiles + i : tiles + i + 1, :] = second[:, LANES * i : LANES * (i + 1)]
        gather_to_all(buf, index)

    def get_sums(buf, index):
        total = arrived(buf, index)
        tiles = total.shape[0] // 2
        return rows_to_vec(total, 0, tiles), rows_to_vec(total, tiles, tiles)

    def moments(buf, index, inv):
        total, squares = get_sums(buf, index)
        mean = total * inv
        var = squares * inv - mean * mean
        return mean, lax.rsqrt(var + EPS)

    zero_n = jnp.zeros((8, narrow), F32)

    grads = (
        (gr_ref, gr_core, gr_got, gr_fin),
        (gs_ref, gs_core, gs_got, gs_fin),
        (ge_ref, ge_core, ge_got, ge_fin),
    )
    lines = clips // 2
    line_me = lax.div(clip, 2)
    peers = frames * lines

    def scatter_cores(index):
        full, pair, _, _ = grads[index]
        half = pair.shape[1]
        view = full.reshape(frames, 2 * half, full.shape[1])
        theirs = pl.ds(pl.multiple_of((1 - core) * half, half), half)
        return pltpu.make_async_remote_copy(
            src_ref=view.at[:, theirs],
            dst_ref=pair,
            send_sem=rs_send.at[index, 0],
            recv_sem=rs_recv.at[index, 0],
            device_id=partner,
            device_id_type=MESH,
        )

    def scatter_chips(index):
        full, pair, got, _ = grads[index]
        scatter_cores(index).wait()
        half, width = pair.shape[1], pair.shape[2]
        mine = pl.ds(pl.multiple_of(core * half, half), half)
        view = full.reshape(frames, 2 * half, width)

        def add(f, carry):
            pair[f] = (pair[f].astype(F32) + view[f, mine, :].astype(F32)).astype(BF16)
            return carry

        lax.fori_loop(0, frames, add, 0)
        cut = width // lines
        slot_me = line_me * frames + frame

        def block(line, owner):
            return pair.at[owner, :, pl.ds(pl.multiple_of(line * cut, LANES), cut)]

        def send(k, carry):
            line = lax.rem(line_me + lax.div(k, frames), lines)
            owner = lax.rem(frame + lax.rem(k, frames), frames)
            pltpu.make_async_remote_copy(
                src_ref=block(line, owner),
                dst_ref=got.at[slot_me],
                send_sem=rs_send.at[index, 1],
                recv_sem=rs_recv.at[index, 1],
                device_id=(line * 2 + core, owner),
                device_id_type=MESH,
            ).start()
            return carry

        lax.fori_loop(1, peers, send, 0)
        own = pltpu.make_async_copy(block(line_me, frame), got.at[slot_me], rs_send.at[index, 2])
        own.start()
        own.wait()

    def gather_owners(index):
        _, pair, got, fin = grads[index]
        half, width = pair.shape[1], pair.shape[2]
        cut = width // lines
        most = got.at[pl.ds(0, peers - 1)]
        pltpu.make_async_copy(most, most, rs_recv.at[index, 1]).wait()
        pltpu.make_async_copy(most, most, rs_send.at[index, 1]).wait()
        spot = fin.at[
            pl.ds(pl.multiple_of(core * half, half), half), pl.ds(pl.multiple_of(line_me * cut, LANES), cut)
        ]
        spot[...] = jnp.sum(got[...].astype(F32), axis=0).astype(BF16)

        def send(k, carry):
            pltpu.make_async_remote_copy(
                src_ref=spot,
                dst_ref=spot,
                send_sem=rs_send.at[index, 2],
                recv_sem=rs_recv.at[index, 2],
                device_id=(lax.rem(clip + k, clips), frame),
                device_id_type=MESH,
            ).start()
            return carry

        lax.fori_loop(1, clips, send, 0)

    def finish_owners(index):
        _, _, got, fin = grads[index]
        most = got.at[pl.ds(0, clips - 1)]
        pltpu.make_async_copy(most, most, rs_recv.at[index, 2]).wait()
        pltpu.make_async_copy(most, most, rs_send.at[index, 2]).wait()
        return fin

    big = rows // 2

    def conv_one(i, carry):
        at = pl.ds(pl.multiple_of(i * big, big), big)
        v = dot(xm[at, :], wr[...])
        pre1[at, :] = v
        return carry[0] + part_sum(v), carry[1] + part_sum(v * v)

    sums = lax.fori_loop(0, 2, conv_one, (zero_n, zero_n))
    send_sums(st1, 1, *sums)
    weight_pass(1)
    mean1, inv1 = moments(st1, 1, inv_n)
    scale1 = inv1 * gain1
    offset1 = bias1 - mean1 * scale1

    def both(v):
        return jnp.concatenate([v] * nar_tiles, axis=1)

    def act_one(i, carry):
        at = block_at(i)
        z = pre1[at, :] * scale1 + offset1
        s = sigmoid(z)
        m = both(mask[at, :])
        ms = m * s
        spad[1, pl.ds(pl.multiple_of(i * BLOCK + pad, 8), BLOCK), :] = ms * z
        slope1[at, :] = ms * (1.0 + z * (1.0 - s))
        return carry

    lax.fori_loop(0, blocks, act_one, 0)

    def spread():
        def shifted(i, carry):
            at = block_at(i)
            v = spad[1, pl.ds(pl.multiple_of(i * BLOCK + pad - 8, 8), BLOCK + 16), :]
            here = pl.ds(pl.multiple_of(i * BLOCK + pad, 8), BLOCK)
            spad[0, here, :] = pltpu.roll(v, 2, 0)[8 : 8 + BLOCK] * both(left_ok[at, :])
            spad[2, here, :] = pltpu.roll(v, BLOCK + 14, 0)[8 : 8 + BLOCK] * both(right_ok[at, :])
            return carry

        lax.fori_loop(0, blocks, shifted, 0)

    def gather_nine(flip):
        def step(i, carry):
            at = block_at(i)
            for tap in range(9):
                row_off, col_off = (tap // 3, tap % 3) if not flip else (2 - tap // 3, 2 - tap % 3)
                src = pl.ds(pl.multiple_of(i * BLOCK + pad * row_off, 8), BLOCK)
                nine[at, narrow * tap : narrow * (tap + 1)] = spad[col_off, src, :].astype(BF16)
            return carry

        lax.fori_loop(0, blocks, step, 0)

    spread()
    gather_nine(False)
    weight_wait(1)

    def conv_two(i, carry):
        at = pl.ds(pl.multiple_of(i * big, big), big)
        v = dot(nine[at, :], ws[...].reshape(9 * narrow, narrow))
        pre2[at, :] = v
        mv = both(mask[at, :]) * v
        return carry[0] + part_sum(mv), carry[1] + part_sum(mv * v)

    sums = lax.fori_loop(0, 2, conv_two, (zero_n, zero_n))
    send_sums(st2, 2, *sums)
    weight_pass(2)
    weight_wait(2)
    wet[...] = we[...].T
    wrt[...] = wr[...].T
    mean2, inv2 = moments(st2, 2, inv_n)
    scale2 = inv2 * gain2
    offset2 = bias2 - mean2 * scale2

    def act_two(i, carry):
        at = block_at(i)
        z = pre2[at, :] * scale2 + offset2
        s = sigmoid(z)
        ms = both(mask[at, :]) * s
        act2[at, :] = (ms * z).astype(BF16)
        slope2[at, :] = ms * (1.0 + z * (1.0 - s))
        return carry

    lax.fori_loop(0, blocks, act_two, 0)

    zero_w = jnp.zeros((8, channels), F32)

    def conv_three(i, carry):
        at = block_at(i)
        v = dot(act2[at, :], we[...])
        pre3[at, :] = v
        return carry[0] + part_sum(v), carry[1] + part_sum(v * v)

    sums = lax.fori_loop(0, blocks, conv_three, (zero_w, zero_w))
    send_sums(st3, 3, *sums)
    for tap in range(9):
        wst[narrow * tap : narrow * (tap + 1), :] = ws[tap].T
    pltpu.make_async_copy(cs, cs, local_sem.at[1]).wait()
    mean3, inv3 = moments(st3, 3, inv_w)
    scale3 = inv3 * gain3
    offset3 = bias3 - mean3 * scale3

    def finish(i, carry):
        at = block_at(i)
        m = mask[at, :]
        first, second = [], []
        for j in range(wide_tiles):
            lanes = slice(LANES * j, LANES * (j + 1))
            p = pre3[at, lanes]
            t = p * scale3[:, lanes] + offset3[:, lanes] + xm[at, lanes].astype(F32)
            s = sigmoid(t)
            ms = m * s
            os_rows[j, at, :] = (ms * t).astype(BF16)
            g = cs_rows[j, at, :].astype(F32) * (ms * (1.0 + t * (1.0 - s)))
            gt[at, lanes] = g
            first.append(part_sum(g))
            second.append(part_sum(g * ((p - mean3[:, lanes]) * inv3[:, lanes])))
        return carry[0] + jnp.concatenate(first, axis=1), carry[1] + jnp.concatenate(second, axis=1)

    sums = lax.fori_loop(0, blocks, finish, (zero_w, zero_w))
    send_sums(st4, 4, *sums)
    for j in range(wide_tiles):
        lanes = pl.ds(LANES * j, LANES)
        pltpu.make_async_copy(os.at[j], out_hbm.at[:, :, lanes], out_sem.at[0]).start()
    shift3, slope_gain3 = get_sums(st4, 4)

    def back_terms(scale, inv, mean, shift_sum, gain_sum, inv_cnt):
        along = scale * inv * gain_sum * inv_cnt
        return along, scale * shift_sum * inv_cnt - mean * along

    along3, flat3 = back_terms(scale3, inv3, mean3, shift3, slope_gain3, inv_w)

    def back_three(i, carry):
        at = block_at(i)
        m = mask[at, :]
        for j in range(wide_tiles):
            lanes = slice(LANES * j, LANES * (j + 1))
            g = gt[at, lanes] * scale3[:, lanes] - pre3[at, lanes] * along3[:, lanes] - m * flat3[:, lanes]
            gp3[at, lanes] = g.astype(BF16)
        return carry

    lax.fori_loop(0, blocks, back_three, 0)

    def back_expand(i, carry):
        at = pl.ds(pl.multiple_of(i * big, big), big)
        d = dot(gp3[at, :], wet[...]) * slope2[at, :]
        dz[at, :] = d
        return carry[0] + part_sum(d), carry[1] + part_sum(d * ((pre2[at, :] - mean2) * inv2))

    sums = lax.fori_loop(0, 2, back_expand, (zero_n, zero_n))
    send_sums(st5, 5, *sums)

    def grad_expand(i, carry):
        lanes = pl.ds(pl.multiple_of(i * 256, 256), 256)
        ge_ref[:, lanes] = dot_tn(act2[...], gp3[:, lanes]).astype(BF16)
        return carry

    lax.fori_loop(0, channels // 256, grad_expand, 0)
    if own_gather:
        scatter_cores(2).start()
    shift2, slope_gain2 = get_sums(st5, 5)
    along2, flat2 = back_terms(scale2, inv2, mean2, shift2, slope_gain2, inv_n)

    def back_two(i, carry):
        at = block_at(i)
        here = pl.ds(pl.multiple_of(i * BLOCK + pad, 8), BLOCK)
        act2[at, :] = spad[1, here, :].astype(BF16)
        m = both(mask[at, :])
        spad[1, here, :] = dz[at, :] * scale2 - m * (pre2[at, :] * along2 + flat2)
        return carry

    lax.fori_loop(0, blocks, back_two, 0)
    spread()
    gather_nine(True)

    def back_spatial(i, carry):
        at = pl.ds(pl.multiple_of(i * big, big), big)
        d = dot(nine[at, :], wst[...]) * slope1[at, :]
        dz[at, :] = d
        return carry[0] + part_sum(d), carry[1] + part_sum(d * ((pre1[at, :] - mean1) * inv1))

    sums = lax.fori_loop(0, 2, back_spatial, (zero_n, zero_n))
    send_sums(st6, 6, *sums)

    def grad_spatial(i, carry):
        lanes = pl.ds(pl.multiple_of(i * narrow, narrow), narrow)
        gs_ref[:, lanes] = dot_tn(act2[...], nine[:, lanes]).astype(BF16)
        return carry

    lax.fori_loop(0, 9, grad_spatial, 0)
    if own_gather:
        scatter_cores(1).start()
        scatter_chips(2)
        scatter_chips(1)
    shift1, slope_gain1 = get_sums(st6, 6)
    along1, flat1 = back_terms(scale1, inv1, mean1, shift1, slope_gain1, inv_n)

    def back_one(i, carry):
        at = block_at(i)
        g = dz[at, :] * scale1 - both(mask[at, :]) * (pre1[at, :] * along1 + flat1)
        gp1[at, :] = g.astype(BF16)
        return carry

    lax.fori_loop(0, blocks, back_one, 0)

    def grad_reduce(i, carry):
        lanes = pl.ds(pl.multiple_of(i * 256, 256), 256)
        gr_ref[lanes, :] = dot_tn(xm[:, lanes], gp1[...]).astype(BF16)
        return carry

    lax.fori_loop(0, channels // 256, grad_reduce, 0)
    if own_gather:
        scatter_cores(0).start()
    pltpu.make_async_copy(os, os, out_sem.at[0]).wait()

    def grad_in(i, carry):
        at = block_at(i)
        m = mask[at, :]
        back = dot(gp1[at, :], wrt[...])
        for j in range(wide_tiles):
            lanes = slice(LANES * j, LANES * (j + 1))
            os_rows[j, at, :] = (m * back[:, lanes] + gt[at, lanes]).astype(BF16)
        return carry

    lax.fori_loop(0, blocks, grad_in, 0)
    for j in range(wide_tiles):
        lanes = pl.ds(LANES * j, LANES)
        pltpu.make_async_copy(os.at[j], gin_hbm.at[:, :, lanes], out_sem.at[1]).start()

    def own_part(ref, v):
        width = ref.shape[0]
        spot = frame * width
        tile = jnp.zeros((1, LANES), F32)
        for t in range(v.shape[1] // LANES):
            tile = jnp.where(lax.div(spot, LANES) == t, v[:, LANES * t : LANES * (t + 1)], tile)
        tile = pltpu.roll(jnp.concatenate([tile] * 8, axis=0), lax.rem(LANES - lax.rem(spot, LANES), LANES), 1)
        ref[...] = tile[0, 0:width]

    own_part(vec1_gain, slope_gain1)
    own_part(vec1_shift, shift1)
    own_part(vec2_gain, slope_gain2)
    own_part(vec2_shift, shift2)
    own_part(vec3_gain, slope_gain3)
    own_part(vec3_shift, shift3)

    if own_gather:
        scatter_chips(0)
        for index in (2, 1, 0):
            gather_owners(index)
        ge_out[...] = finish_owners(2)[...].astype(F32)
        fin = finish_owners(1)
        for tap in range(9):
            gs_out[tap] = fin[:, narrow * tap : narrow * (tap + 1)].astype(F32)
        gr_out[...] = finish_owners(0)[...].astype(F32)
    else:
        gr_out[...] = gr_ref[...]
        gs_out[...] = gs_ref[...]
        ge_out[...] = ge_ref[...]
    pltpu.make_async_copy(os, os, out_sem.at[1]).wait()


def on_device(
    dims,
    x_in,
    cotangent,
    w_reduce,
    w_spatial,
    w_expand,
    gain_one,
    shift_one,
    gain_two,
    shift_two,
    gain_three,
    shift_three,
    bucket,
    frame_count,
):
    clips, frames = dims
    slots, side, _, channels = x_in.shape
    narrow = w_reduce.shape[1]
    pixels = side * side
    rows = pixels * slots
    tiles = channels // LANES
    devices = clips * frames
    own_gather = all(n % 32 == 0 for n in (w_reduce.shape[0], w_spatial.shape[2], w_expand.shape[0]))
    w_spatial = w_spatial.reshape(9, -1, narrow)
    if not own_gather:
        w_reduce = lax.all_gather(w_reduce, "frame", axis=0, tiled=True)
        w_spatial = lax.all_gather(w_spatial, "frame", axis=1, tiled=True)
        w_expand = lax.all_gather(w_expand, "frame", axis=0, tiled=True)

    def by_pixel(v):
        return jnp.transpose(v, (1, 2, 0, 3)).reshape(pixels, slots, channels)

    any_spec = pl.BlockSpec(memory_space=pl.ANY)
    vmem = pl.BlockSpec(memory_space=pltpu.VMEM)
    smem = pl.BlockSpec(memory_space=pltpu.SMEM)
    big = jax.ShapeDtypeStruct((pixels, slots, channels), BF16)
    staged = pltpu.VMEM((tiles, pixels, slots, LANES), BF16)
    narrow_f32 = pltpu.VMEM((rows, narrow), F32)
    wide_f32 = pltpu.VMEM((rows, channels), F32)
    lanes_f32 = pltpu.VMEM((rows, LANES), F32)

    def stats(count):
        return pltpu.VMEM((devices, count, LANES), F32)

    def pieces(part, width, lead):
        half, lines = part // 2, clips // 2
        if lead == 0:
            return pltpu.VMEM((frames, half, width), BF16)
        if lead == 1:
            return pltpu.VMEM((frames * lines, half, width // lines), BF16)
        return pltpu.VMEM((part, width), BF16)

    if own_gather:
        parts = ((channels // frames, narrow), (narrow // frames, 9 * narrow), (narrow // frames, channels))
        grad_shapes = (
            jax.ShapeDtypeStruct((channels // frames, narrow), F32),
            jax.ShapeDtypeStruct((9, narrow // frames, narrow), F32),
            jax.ShapeDtypeStruct((narrow // frames, channels), F32),
        )
    else:
        parts = ((32, 256),) * 3
        grad_shapes = (
            jax.ShapeDtypeStruct((channels, narrow), BF16),
            jax.ShapeDtypeStruct((narrow, 9 * narrow), BF16),
            jax.ShapeDtypeStruct((narrow, channels), BF16),
        )
    piece_scratch = [pieces(part, width, lead) for lead in range(3) for part, width in parts]

    out, gin, gr, gs, ge, *vectors = pl.pallas_call(
        functools.partial(block_kernel, (clips, frames, side, own_gather)),
        out_shape=(
            big,
            big,
            *grad_shapes,
            *(jax.ShapeDtypeStruct((narrow // frames,), F32),) * 4,
            *(jax.ShapeDtypeStruct((channels // frames,), F32),) * 2,
        ),
        in_specs=[any_spec] * 5 + [vmem] * 6 + [smem] * 2,
        out_specs=(any_spec, any_spec) + (vmem,) * 9,
        scratch_shapes=[
            staged,
            staged,
            staged,
            pltpu.VMEM((rows, channels), BF16),
            lanes_f32,
            lanes_f32,
            lanes_f32,
            pltpu.VMEM((channels, narrow), BF16),
            pltpu.VMEM((9, narrow, narrow), BF16),
            pltpu.VMEM((narrow, channels), BF16),
            pltpu.VMEM((9 * narrow, narrow), BF16),
            pltpu.VMEM((channels, narrow), BF16),
            pltpu.VMEM((narrow, channels), BF16),
            narrow_f32,
            narrow_f32,
            narrow_f32,
            narrow_f32,
            narrow_f32,
            pltpu.VMEM((3, rows + 4 * side, narrow), F32),
            pltpu.VMEM((rows, narrow), BF16),
            pltpu.VMEM((rows, 9 * narrow), BF16),
            wide_f32,
            wide_f32,
            pltpu.VMEM((rows, channels), BF16),
            pltpu.VMEM((rows, narrow), BF16),
            stats(8),
            stats(2 * narrow // LANES),
            stats(2 * narrow // LANES),
            stats(2 * tiles),
            stats(2 * tiles),
            stats(2 * narrow // LANES),
            stats(2 * narrow // LANES),
            pltpu.SemaphoreType.DMA((5,)),
            pltpu.SemaphoreType.DMA((3, frames)),
            pltpu.SemaphoreType.DMA((3, frames)),
            pltpu.SemaphoreType.DMA((3, frames)),
            pltpu.SemaphoreType.DMA((3, frames)),
            pltpu.SemaphoreType.DMA((7,)),
            pltpu.SemaphoreType.DMA((7,)),
            pltpu.SemaphoreType.DMA((2,)),
            pltpu.VMEM((channels, narrow), BF16),
            pltpu.VMEM((narrow, 9 * narrow), BF16),
            pltpu.VMEM((narrow, channels), BF16),
            *piece_scratch,
            pltpu.SemaphoreType.DMA((3, 3)),
            pltpu.SemaphoreType.DMA((3, 3)),
        ],
        compiler_params=pltpu.CompilerParams(
            collective_id=0, has_side_effects=True, vmem_limit_bytes=58 * 1024 * 1024
        ),
    )(
        by_pixel(x_in),
        by_pixel(cotangent),
        w_reduce,
        w_spatial,
        w_expand,
        gain_one,
        shift_one,
        gain_two,
        shift_two,
        gain_three,
        shift_three,
        bucket,
        frame_count,
    )

    def by_frame(v):
        return jnp.transpose(v.reshape(side, side, slots, channels), (2, 0, 1, 3))

    def owned(v):
        part = lax.psum_scatter(v, "frame", scatter_dimension=0, tiled=True)
        return lax.psum(part, "clip").astype(F32)

    if not own_gather:
        gr, gs, ge = owned(gr), owned(gs), owned(ge)
        gs = gs.reshape(-1, 9, narrow).transpose(1, 0, 2)
    return (by_frame(out), by_frame(gin), gr, gs.reshape(3, 3, -1, narrow), ge, *vectors)


def solution(mesh):
    by_device = P(("clip", "frame"))
    shard = P("frame")
    spatial = P(None, None, "frame", None)
    return jax.shard_map(
        functools.partial(on_device, (mesh.shape["clip"], mesh.shape["frame"])),
        mesh=mesh,
        in_specs=(by_device, by_device, shard, spatial) + (shard,) * 7 + (by_device, by_device),
        out_specs=(by_device, by_device, shard, spatial) + (shard,) * 7,
        check_vma=False,
    )
```

time: 621 us -> 126 us (0.20)
  blocking collectives: 360 us -> 0 us
  waiting for transfers between devices: 166 us -> 0 us
  Pallas kernels: 0 us -> 114 us
  matrix products: 31.9 us -> 0 us
  other arithmetic: 29.2 us -> 0 us
  between operations: 15.5 us -> 1.37 us
    psum x6 -> x0, blocking collectives: 237 us -> none  [the longest x3 120 us: norm_back(): lax.psum((jnp.sum(grad_z, axis=(0, 1, 2)), jnp.sum(grad_z * scaled, axis=...]
    reduce_scatter x3 -> x0, waiting for transfers between devices: 144 us -> none  [the longest x1 67.5 us: on_device(): lax.psum_scatter(grad_spatial.astype(jnp.bfloat16), 'frame', scatter_dime...]
    pallas_call x0 -> x1, Pallas kernels: none -> 114 us  [on_device(): pl.pallas_call(functools.partial(block_kernel, (clips, frames, side, own_...]
    all_gather x4 -> x0, blocking collectives: 99.7 us -> none  [the longest x1 33.5 us: on_device(): lax.all_gather(local_params[2], 'frame', axis=0, tiled=True)]
    dot_general x33 -> x0, matrix products: 31.9 us -> none  [the longest x9 5.78 us: spatial_forward(): jnp.einsum('fhwc,cd->fhwd', window, kernel[row_off, col_off], preferred_e...]
    unnamed x1 -> x0, blocking collectives: 23.2 us -> none
    psum x1 -> x0, waiting for transfers between devices: 21.4 us -> none  [on_device(): lax.psum(owned[0].astype(jnp.bfloat16), 'clip').astype(jnp.float32)]
    convert_element_type x14 -> x0, other arithmetic: 13.9 us -> none  [the longest x3 8.78 us: norm_back(): return (grad_pre.astype(jnp.bfloat16), gain_grad, shift_grad)]
  transfers between devices with their start and end apart: 5 -> 0, of which waited for: 4 -> 0; matrix products, arithmetic and copies ran while one was open for 5% -> 0% of each run, Pallas kernels for 0% -> 0%
where the time goes in v1:
time: 126 us
  Pallas kernels  114 us (90%)
  local copies, waits for them, and re-layouts  10.4 us (8%)
  between operations  1.37 us (1%)
    pallas_call x1, Pallas kernels, on_device(): pl.pallas_call(functools.partial(block_kernel, (clips, frames, side, own_...  114 us
    unnamed x31, local copies, waits for them, and re-layouts  10.4 us

profile of v1, /device:TPU:0, one launch (start us, length us, event | category | flops | bytes accessed | tf_op | source)
XLA Modules:
  0.0 125.9 jit_solution(14890386189699636588)
XLA Ops:
  1.3 114.1 %shard_map.212 = (bf16[400,2,1024]{2,1,0:T(2,128)(2,1)}, bf16[400,2,1024]{2,1,0:T(2,128)(2,1)}, f32[128,256]{1,0:T(8,128)}, f32[9,32,256]{2,1,0:T(8,128)}, f32[3...) custom-call(bf16[400,2,1024]{2,1,0:T(2,128)(2,1)} %bitcast.14, ...), custom_call_target="tpu_custom_call" | custom-call | tf_op jit(solution)/shard_map/pallas_call | solution.py:782
  115.4 0.0 copy-start
  115.4 4.1 %copy.36 = bf16[2,20,20,1024]{3,0,2,1:T(2,128)(2,1)} copy(bf16[2,20,20,1024]{3,0,2,1:T(2,128)(2,1)} %bitcast.17) | data formatting | bytes 3276800
  119.6 0.0 copy-done
  119.6 0.0 copy-start.3
  119.6 0.0 copy-start.1
  119.6 0.0 copy-start.2
  119.6 0.0 copy-start.9
  119.6 0.0 copy-start.8
  119.6 0.0 copy-start.7
  119.6 0.0 copy-start.6
  119.6 0.0 copy-start.5
  119.6 0.0 copy-start.4
  119.6 1.2 copy.37
  120.8 0.0 copy-done.3
  120.8 0.7 copy.38
  121.5 0.0 copy-done.1
  121.5 0.7 copy.39
  122.2 0.0 copy-done.2
  122.2 0.7 copy.40
  122.9 0.0 copy-done.9
  122.9 0.5 copy.41
  123.4 0.0 copy-done.8
  123.4 0.5 copy.42
  123.9 0.0 copy-done.7
  123.9 0.5 copy.43
  124.4 0.0 copy-done.6
  124.4 0.5 copy.44
  124.9 0.0 copy-done.5
  124.9 0.5 copy.45
  125.4 0.0 copy-done.4
  125.4 0.5 copy.46
Async XLA Ops:
  115.4 4.1 %copy-start = (bf16[400,2,1024]{2,1,0:T(2,128)(2,1)S(1)}, bf16[400,2,1024]{2,1,0:T(2,128)(2,1)}, u32[]{:S(2)}) copy-start(bf16[400,2,1024]{2,1,0:T(2,128)(2,1)} %get-tuple-element.23) | copy-start | bytes 4915204
  119.6 1.2 copy-start.3
  119.6 1.9 %copy-start.1 = (f32[9,32,256]{2,1,0:T(8,128)S(1)}, f32[9,32,256]{2,1,0:T(8,128)}, u32[]{:S(2)}) copy-start(f32[9,32,256]{2,1,0:T(8,128)} %get-tuple-element.25) | copy-start | bytes 884740
  119.6 2.6 %copy-start.2 = (f32[32,1024]{1,0:T(8,128)S(1)}, f32[32,1024]{1,0:T(8,128)}, u32[]{:S(2)}) copy-start(f32[32,1024]{1,0:T(8,128)} %get-tuple-element.48) | copy-start | bytes 393220
  119.6 3.3 %copy-start.9 = (f32[32]{0:T(128)S(1)}, f32[32]{0:T(128)}, u32[]{:S(2)}) copy-start(f32[32]{0:T(128)} %get-tuple-element.49) | copy-start | bytes 388
  119.6 3.8 %copy-start.8 = (f32[32]{0:T(128)S(1)}, f32[32]{0:T(128)}, u32[]{:S(2)}) copy-start(f32[32]{0:T(128)} %get-tuple-element.50) | copy-start | bytes 388
  119.6 4.3 %copy-start.7 = (f32[32]{0:T(128)S(1)}, f32[32]{0:T(128)}, u32[]{:S(2)}) copy-start(f32[32]{0:T(128)} %get-tuple-element.51) | copy-start | bytes 388
  119.6 4.8 %copy-start.6 = (f32[32]{0:T(128)S(1)}, f32[32]{0:T(128)}, u32[]{:S(2)}) copy-start(f32[32]{0:T(128)} %get-tuple-element.52) | copy-start | bytes 388
  119.6 5.3 %copy-start.5 = (f32[128]{0:T(128)S(1)}, f32[128]{0:T(128)}, u32[]{:S(2)}) copy-start(f32[128]{0:T(128)} %get-tuple-element.53) | copy-start | bytes 1540
  119.6 5.8 %copy-start.4 = (f32[128]{0:T(128)S(1)}, f32[128]{0:T(128)}, u32[]{:S(2)}) copy-start(f32[128]{0:T(128)} %get-tuple-element.54) | copy-start | bytes 1540

commit v2 on v1

v2 whole, which is shorter than its diff:
```python
import functools

import jax
import jax.numpy as jnp
from jax import lax
from jax.experimental import pallas as pl
from jax.experimental.pallas import tpu as pltpu
from jax.sharding import PartitionSpec as P

SMALL_SIDE = 14
EPS = 1e-05
LANES = 128
BLOCK = 80
MESH = pl.DeviceIdType.MESH
X_FIRST = (False, True, False, True, True)
F32 = jnp.float32
BF16 = jnp.bfloat16


def sigmoid(v):
    return 0.5 * jnp.tanh(0.5 * v) + 0.5


def part_sum(v):
    rows, width = v.shape
    return jnp.sum(v.reshape(rows // 8, 8, width), axis=0)


def dot(a, b):
    return jnp.dot(a, b, preferred_element_type=F32)


def rows_to_vec(tile, first, count):
    return jnp.concatenate([tile[first + i : first + i + 1] for i in range(count)], axis=1)


def block_kernel(
    dims,
    x_hbm,
    ct_hbm,
    wr_hbm,
    ws_hbm,
    we_hbm,
    g1_ref,
    b1_ref,
    g2_ref,
    b2_ref,
    g3_ref,
    b3_ref,
    bucket_ref,
    count_ref,
    out_hbm,
    gin_hbm,
    gr_out,
    gs_out,
    ge_out,
    vec1_gain,
    vec1_shift,
    vec2_gain,
    vec2_shift,
    vec3_gain,
    vec3_shift,
    xs,
    cs,
    os,
    x_rows,
    ct_rows,
    out_rows,
    xm,
    xt,
    a1t,
    a2t,
    mask,
    left_ok,
    right_ok,
    wr,
    ws,
    we,
    wst,
    wet,
    wrt,
    pre1,
    slope1,
    pre2,
    slope2,
    dz,
    spad,
    act2,
    nine,
    pre3,
    gt,
    gp3,
    gp1,
    par,
    counts,
    st1,
    st2,
    st3,
    st4,
    st5,
    st6,
    local_sem,
    wsend,
    wrecv,
    st_send,
    st_recv,
    out_sem,
    rs_send,
    rs_recv,
    *unit_refs,
):
    clips, frames, side, own_gather = dims
    units = len(X_FIRST)
    full_refs, pair_refs, mid_refs, got_refs, fin_refs = [unit_refs[units * i : units * (i + 1)] for i in range(5)]
    gr_ref, *gs_refs, ge_ref = full_refs
    devices = clips * frames
    clip = lax.axis_index("clip")
    frame = lax.axis_index("frame")
    me = clip * frames + frame
    core = lax.rem(clip, 2)
    partner = (clip + 1 - 2 * core, frame)
    rows = xm.shape[0]
    channels = xm.shape[1]
    narrow = wr.shape[1]
    wide_tiles = channels // LANES
    nar_tiles = narrow // LANES
    blocks = rows // BLOCK
    pad = 2 * side

    def other(k):
        return (lax.rem(clip + lax.div(k, frames), clips), lax.rem(frame + lax.rem(k, frames), frames))

    for j in range(wide_tiles):
        lanes = pl.ds(LANES * j, LANES)
        pltpu.make_async_copy(x_hbm.at[:, :, lanes], xs.at[j], local_sem.at[0]).start()
    if own_gather:
        part_r = wr_hbm.shape[0]
        part_s = ws_hbm.shape[1]
        part_e = we_hbm.shape[0]
        own_r = wr.at[pl.ds(pl.multiple_of(frame * part_r, part_r), part_r)]
        own_s = ws.at[:, pl.ds(pl.multiple_of(frame * part_s, part_s), part_s)]
        own_e = we.at[pl.ds(pl.multiple_of(frame * part_e, part_e), part_e)]
    else:
        own_r, own_s, own_e = wr, ws, we
    own_copies = [
        pltpu.make_async_copy(wr_hbm, own_r, local_sem.at[2]),
        pltpu.make_async_copy(ws_hbm, own_s, local_sem.at[3]),
        pltpu.make_async_copy(we_hbm, own_e, local_sem.at[4]),
    ]
    for copy in own_copies:
        copy.start()
    for j in range(wide_tiles):
        lanes = pl.ds(LANES * j, LANES)
        pltpu.make_async_copy(ct_hbm.at[:, :, lanes], cs.at[j], local_sem.at[1]).start()

    def copies_in(staged, index):
        return pltpu.make_async_copy(staged, staged, local_sem.at[index])

    def to_rows(staged, native, index):
        return pltpu.make_async_copy(staged.reshape(wide_tiles, rows, LANES), native, local_sem.at[index])

    barrier = pltpu.get_barrier_semaphore()

    def greet(k, carry):
        pl.semaphore_signal(barrier, inc=1, device_id=other(k), device_id_type=MESH)
        return carry

    lax.fori_loop(1, devices, greet, 0)

    row_id = lax.broadcasted_iota(jnp.int32, (rows, LANES), 0)
    pixel = row_id >> 1
    slot = row_id & 1
    line = (pixel * 3277) >> 16
    col = pixel - line * side
    extent = [jnp.where(bucket_ref[f] == 0, SMALL_SIDE, side) for f in range(2)]
    limit = [jnp.where(count_ref[0] > f, extent[f], 0) for f in range(2)]
    bound = jnp.where(slot == 0, limit[0], limit[1])
    live = ((line < bound) & (col < bound)).astype(F32)
    mask[...] = live
    left_ok[...] = (col >= 1).astype(F32)
    right_ok[...] = (col <= side - 2).astype(F32)

    par[frame] = jnp.zeros((8, LANES), F32)
    for i, ref in enumerate((g1_ref, b1_ref, g2_ref, b2_ref, g3_ref, b3_ref)):
        width = ref.shape[0]
        par[frame, i : i + 1, 0:width] = ref[...].astype(F32).reshape(1, width)
    counts[me] = jnp.sum(live, axis=0, keepdims=True)

    copies_in(xs, 0).wait()
    to_rows(xs, x_rows, 0).start()
    to_rows(xs, x_rows, 0).wait()

    def block_at(i):
        return pl.ds(pl.multiple_of(i * BLOCK, BLOCK), BLOCK)

    def mask_in(i, carry):
        at = block_at(i)
        m = mask[at, :].astype(BF16)
        for j in range(wide_tiles):
            xm[at, LANES * j : LANES * (j + 1)] = x_rows[j, at, :] * m
        return carry

    lax.fori_loop(0, blocks, mask_in, 0)
    edge = jnp.zeros((3, pad, narrow), F32)
    spad[:, 0:pad, :] = edge
    spad[:, pad + rows : 2 * pad + rows, :] = edge
    for copy in own_copies:
        copy.wait()

    pl.semaphore_wait(barrier, devices - 1)

    def gather_to_all(buf, index):
        for a in range(clips):
            to_clip = lax.rem(clip + a, clips)

            def send(b, carry):
                pltpu.make_async_remote_copy(
                    src_ref=buf.at[me],
                    dst_ref=buf.at[me],
                    send_sem=st_send.at[index],
                    recv_sem=st_recv.at[index],
                    device_id=(to_clip, lax.rem(frame + b, frames)),
                    device_id_type=MESH,
                ).start()
                return carry

            lax.fori_loop(0 if a else 1, frames, send, 0)

    def arrived(buf, index):
        most = buf.at[pl.ds(0, devices - 1)]
        pltpu.make_async_copy(most, most, st_recv.at[index]).wait()
        pltpu.make_async_copy(most, most, st_send.at[index]).wait()
        return jnp.sum(buf[...], axis=0)

    across = lax.rem(frame, 2)
    along = lax.div(frame, 2)
    depth = frames // 2
    x_peer = (clip, along * 2 + 1 - across)

    def owner_at(d, side_x):
        return lax.rem(along - d + depth, depth) * 2 + side_x

    if own_gather:

        def halves(ref, axis, part):
            half = part // 2

            def view(owner):
                at = pl.ds(pl.multiple_of(owner * part + core * half, half), half)
                return ref.at[at] if axis == 0 else ref.at[:, at]

            return view

        views = (halves(wr, 0, part_r), halves(ws, 1, part_s), halves(we, 0, part_e))

        def weight_copy(index, hop, d, owner, target):
            part = views[index](owner)
            return pltpu.make_async_remote_copy(
                src_ref=part,
                dst_ref=part,
                send_sem=wsend.at[index, hop, d],
                recv_sem=wrecv.at[index, hop, d],
                device_id=target,
                device_id_type=MESH,
            )

        def along_z(index):
            for d in range(1, depth):
                target = (clip, lax.rem(along + d, depth) * 2 + across)
                weight_copy(index, 0, d, frame, target).start()

        def along_x(index, d):
            if d:
                weight_copy(index, 0, d, owner_at(d, across), x_peer).wait_recv()
            weight_copy(index, 1, d, owner_at(d, across), x_peer).start()

        def to_core(index, d):
            if d:
                weight_copy(index, 2, d, owner_at(d, across), partner).start()

        def to_core_late(index, d):
            owner = owner_at(d, 1 - across)
            weight_copy(index, 1, d, owner, partner).wait_recv()
            weight_copy(index, 3, d, owner, partner).start()

        def weight_ready(index):
            for d in range(depth):
                if d:
                    weight_copy(index, 2, d, owner_at(d, across), partner).wait_recv()
                weight_copy(index, 3, d, owner_at(d, 1 - across), partner).wait_recv()

        def weight_sent(index):
            for d in range(depth):
                if d:
                    weight_copy(index, 0, d, frame, partner).wait_send()
                    weight_copy(index, 2, d, frame, partner).wait_send()
                weight_copy(index, 1, d, frame, partner).wait_send()
                weight_copy(index, 3, d, frame, partner).wait_send()

    else:

        def nothing(*args):
            pass

        along_z = along_x = to_core = to_core_late = weight_ready = weight_sent = nothing

    def send_params():
        def send(b, carry):
            pltpu.make_async_remote_copy(
                src_ref=par.at[frame],
                dst_ref=par.at[frame],
                send_sem=st_send.at[0],
                recv_sem=st_recv.at[0],
                device_id=(clip, lax.rem(frame + b, frames)),
                device_id_type=MESH,
            ).start()
            return carry

        lax.fori_loop(1, frames, send, 0)

    along_z(0)
    along_x(0, 0)
    along_z(1)
    along_x(1, 0)
    gather_to_all(counts, 7)
    send_params()
    for d in range(1, depth):
        along_x(0, d)
        to_core(0, d)
    for d in range(depth):
        to_core_late(0, d)

    weight_ready(0)

    def send_sums(buf, index, first, second):
        tiles = first.shape[1] // LANES
        first = jnp.sum(first, axis=0, keepdims=True)
        second = jnp.sum(second, axis=0, keepdims=True)
        for i in range(tiles):
            buf[me, i : i + 1, :] = first[:, LANES * i : LANES * (i + 1)]
            buf[me, tiles + i : tiles + i + 1, :] = second[:, LANES * i : LANES * (i + 1)]
        gather_to_all(buf, index)

    def get_sums(buf, index):
        total = arrived(buf, index)
        tiles = total.shape[0] // 2
        return rows_to_vec(total, 0, tiles), rows_to_vec(total, tiles, tiles)

    def moments(buf, index, inv):
        total, squares = get_sums(buf, index)
        mean = total * inv
        var = squares * inv - mean * mean
        return mean, lax.rsqrt(var + EPS)

    zero_n = jnp.zeros((8, narrow), F32)

    lines = clips // 2
    line_me = lax.div(clip, 2)
    peers = frames
    y_peer = (lax.rem(clip + 2, clips), frame)

    def unit_copy(unit, stage, src, dst, target):
        return pltpu.make_async_remote_copy(
            src_ref=src,
            dst_ref=dst,
            send_sem=rs_send.at[unit, stage],
            recv_sem=rs_recv.at[unit, stage],
            device_id=target,
            device_id_type=MESH,
        )

    def columns(line, cut):
        return pl.ds(pl.multiple_of(line * cut, LANES), cut)

    def cores(unit):
        full, pair = full_refs[unit], pair_refs[unit]
        half = pair.shape[1]
        view = full.reshape(frames, 2 * half, full.shape[1])
        theirs = pl.ds(pl.multiple_of((1 - core) * half, half), half)
        return unit_copy(unit, 0, view.at[:, theirs], pair, partner)

    def near_copy(unit):
        pair, mid = pair_refs[unit], mid_refs[unit]
        half, width = pair.shape[1], pair.shape[2]
        if X_FIRST[unit]:
            return unit_copy(unit, 1, pair.reshape(depth, 2, half, width).at[:, 1 - across], mid, x_peer)
        return unit_copy(unit, 1, pair.at[:, :, columns(1 - line_me, width // lines)], mid, y_peer)

    def near(unit):
        full, pair = full_refs[unit], pair_refs[unit]
        cores(unit).wait()
        half = pair.shape[1]
        mine = pl.ds(pl.multiple_of(core * half, half), half)
        view = full.reshape(frames, 2 * half, full.shape[1])

        def add(f, carry):
            pair[f] = (pair[f].astype(F32) + view[f, mine, :].astype(F32)).astype(BF16)
            return carry

        lax.fori_loop(0, frames, add, 0)
        near_copy(unit).start()

    def far(unit):
        pair, mid, got = pair_refs[unit], mid_refs[unit], got_refs[unit]
        cut = pair.shape[2] // lines
        near_copy(unit).wait()

        def add(k, carry):
            own = pair[2 * k + across] if X_FIRST[unit] else pair[k, :, columns(line_me, cut)]
            mid[k] = (mid[k].astype(F32) + own.astype(F32)).astype(BF16)
            return carry

        lax.fori_loop(0, mid.shape[0], add, 0)
        if X_FIRST[unit]:
            slot_me = line_me * depth + along
            got[slot_me] = mid[along, :, columns(line_me, cut)]

            def send(k, carry):
                line = lax.rem(line_me + lax.div(k, depth), lines)
                deep = lax.rem(along + lax.rem(k, depth), depth)
                src = mid.at[deep, :, columns(line, cut)]
                unit_copy(unit, 2, src, got.at[slot_me], (line * 2 + core, deep * 2 + across)).start()
                return carry

        else:
            got[frame] = mid[frame]

            def send(k, carry):
                owner = lax.rem(frame + k, frames)
                unit_copy(unit, 2, mid.at[owner], got.at[frame], (clip, owner)).start()
                return carry

        lax.fori_loop(1, peers, send, 0)

    def owners(unit):
        got, fin = got_refs[unit], fin_refs[unit]
        half, cut = got.shape[1], got.shape[2]
        most = got.at[pl.ds(0, peers - 1)]
        unit_copy(unit, 2, most, most, partner).wait()
        spot = fin.at[pl.ds(pl.multiple_of(core * half, half), half), columns(line_me, cut)]
        spot[...] = jnp.sum(got[...].astype(F32), axis=0).astype(BF16)

        def send(k, carry):
            unit_copy(unit, 3, spot, spot, (lax.rem(clip + k, clips), frame)).start()
            return carry

        lax.fori_loop(1, clips, send, 0)

    def finished(unit):
        most = got_refs[unit].at[pl.ds(0, clips - 1)]
        unit_copy(unit, 3, most, most, partner).wait()
        return fin_refs[unit]

    big = rows // 2

    def conv_one(i, carry):
        at = pl.ds(pl.multiple_of(i * big, big), big)
        v = dot(xm[at, :], wr[...])
        pre1[at, :] = v
        return carry[0] + part_sum(v), carry[1] + part_sum(v * v)

    sums = lax.fori_loop(0, 2, conv_one, (zero_n, zero_n))
    send_sums(st1, 1, *sums)
    for d in range(1, depth):
        along_x(1, d)
        to_core(1, d)
    along_z(2)
    along_x(2, 0)
    for d in range(depth):
        to_core_late(1, d)
    xt[...] = xm[...].T

    most = par.at[pl.ds(0, frames - 1)]
    pltpu.make_async_copy(most, most, st_recv.at[0]).wait()
    pltpu.make_async_copy(most, most, st_send.at[0]).wait()
    part_n = g1_ref.shape[0]
    part_w = g3_ref.shape[0]
    acc_n = [jnp.zeros((8, LANES), F32) for _ in range(nar_tiles)]
    acc_w = [jnp.zeros((8, LANES), F32) for _ in range(wide_tiles)]
    for f in range(frames):
        tile = par[f]
        spot = f * part_n
        shift = spot % LANES
        acc_n[spot // LANES] += pltpu.roll(tile, shift, 1) if shift else tile
        spot = f * part_w
        shift = spot % LANES
        acc_w[spot // LANES] += pltpu.roll(tile, shift, 1) if shift else tile
    gain1, bias1, gain2, bias2 = [jnp.concatenate([a[i : i + 1] for a in acc_n], axis=1) for i in range(4)]
    gain3, bias3 = [jnp.concatenate([a[i : i + 1] for a in acc_w], axis=1) for i in (4, 5)]
    inv_count = 1.0 / arrived(counts, 7)
    inv_n = jnp.concatenate([inv_count] * nar_tiles, axis=1)
    inv_w = jnp.concatenate([inv_count] * wide_tiles, axis=1)

    mean1, inv1 = moments(st1, 1, inv_n)
    scale1 = inv1 * gain1
    offset1 = bias1 - mean1 * scale1

    def both(v):
        return jnp.concatenate([v] * nar_tiles, axis=1)

    def act_one(i, carry):
        at = block_at(i)
        z = pre1[at, :] * scale1 + offset1
        s = sigmoid(z)
        m = both(mask[at, :])
        ms = m * s
        spad[1, pl.ds(pl.multiple_of(i * BLOCK + pad, 8), BLOCK), :] = ms * z
        slope1[at, :] = ms * (1.0 + z * (1.0 - s))
        return carry

    lax.fori_loop(0, blocks, act_one, 0)

    def spread():
        def shifted(i, carry):
            at = block_at(i)
            v = spad[1, pl.ds(pl.multiple_of(i * BLOCK + pad - 8, 8), BLOCK + 16), :]
            here = pl.ds(pl.multiple_of(i * BLOCK + pad, 8), BLOCK)
            spad[0, here, :] = pltpu.roll(v, 2, 0)[8 : 8 + BLOCK] * both(left_ok[at, :])
            spad[2, here, :] = pltpu.roll(v, BLOCK + 14, 0)[8 : 8 + BLOCK] * both(right_ok[at, :])
            return carry

        lax.fori_loop(0, blocks, shifted, 0)

    def gather_nine(flip):
        def step(i, carry):
            at = block_at(i)
            for tap in range(9):
                row_off, col_off = (tap // 3, tap % 3) if not flip else (2 - tap // 3, 2 - tap % 3)
                src = pl.ds(pl.multiple_of(i * BLOCK + pad * row_off, 8), BLOCK)
                nine[at, narrow * tap : narrow * (tap + 1)] = spad[col_off, src, :].astype(BF16)
            return carry

        lax.fori_loop(0, blocks, step, 0)

    spread()
    gather_nine(False)
    weight_ready(1)
    for d in range(1, depth):
        along_x(2, d)
        to_core(2, d)

    def conv_two(i, carry):
        at = pl.ds(pl.multiple_of(i * big, big), big)
        v = dot(nine[at, :], ws[...].reshape(9 * narrow, narrow))
        pre2[at, :] = v
        mv = both(mask[at, :]) * v
        return carry[0] + part_sum(mv), carry[1] + part_sum(mv * v)

    sums = lax.fori_loop(0, 2, conv_two, (zero_n, zero_n))
    send_sums(st2, 2, *sums)
    wrt[...] = wr[...].T
    a1t[...] = spad[1, pad : pad + rows, :].astype(BF16).T
    for d in range(depth):
        to_core_late(2, d)

    mean2, inv2 = moments(st2, 2, inv_n)
    scale2 = inv2 * gain2
    offset2 = bias2 - mean2 * scale2

    def act_two(i, carry):
        at = block_at(i)
        z = pre2[at, :] * scale2 + offset2
        s = sigmoid(z)
        ms = both(mask[at, :]) * s
        act2[at, :] = (ms * z).astype(BF16)
        slope2[at, :] = ms * (1.0 + z * (1.0 - s))
        return carry

    lax.fori_loop(0, blocks, act_two, 0)

    weight_ready(2)
    zero_w = jnp.zeros((8, channels), F32)

    wide = 2 * BLOCK

    def conv_three(i, carry):
        at = pl.ds(pl.multiple_of(i * wide, wide), wide)
        v = dot(act2[at, :], we[...])
        pre3[at, :] = v
        return carry[0] + part_sum(v), carry[1] + part_sum(v * v)

    sums = lax.fori_loop(0, rows // wide, conv_three, (zero_w, zero_w))
    send_sums(st3, 3, *sums)
    for tap in range(9):
        wst[narrow * tap : narrow * (tap + 1), :] = ws[tap].T
    wet[...] = we[...].T
    a2t[...] = act2[...].T
    copies_in(cs, 1).wait()
    to_rows(cs, ct_rows, 1).start()
    to_rows(cs, ct_rows, 1).wait()
    mean3, inv3 = moments(st3, 3, inv_w)
    scale3 = inv3 * gain3
    offset3 = bias3 - mean3 * scale3

    def from_rows():
        return pltpu.make_async_copy(out_rows, os.reshape(wide_tiles, rows, LANES), out_sem.at[2])

    def send_out(ref, index):
        for j in range(wide_tiles):
            lanes = pl.ds(LANES * j, LANES)
            pltpu.make_async_copy(os.at[j], ref.at[:, :, lanes], out_sem.at[index]).start()

    def finish(i, carry):
        at = block_at(i)
        m = mask[at, :]
        first, second = [], []
        for j in range(wide_tiles):
            lanes = slice(LANES * j, LANES * (j + 1))
            p = pre3[at, lanes]
            t = p * scale3[:, lanes] + offset3[:, lanes] + xm[at, lanes].astype(F32)
            s = sigmoid(t)
            ms = m * s
            out_rows[j, at, :] = (ms * t).astype(BF16)
            g = ct_rows[j, at, :].astype(F32) * (ms * (1.0 + t * (1.0 - s)))
            gt[at, lanes] = g
            first.append(part_sum(g))
            second.append(part_sum(g * ((p - mean3[:, lanes]) * inv3[:, lanes])))
        return carry[0] + jnp.concatenate(first, axis=1), carry[1] + jnp.concatenate(second, axis=1)

    sums = lax.fori_loop(0, blocks, finish, (zero_w, zero_w))
    send_sums(st4, 4, *sums)
    from_rows().start()
    from_rows().wait()
    send_out(out_hbm, 0)
    shift3, slope_gain3 = get_sums(st4, 4)

    def back_terms(scale, inv, mean, shift_sum, gain_sum, inv_cnt):
        along = scale * inv * gain_sum * inv_cnt
        return along, scale * shift_sum * inv_cnt - mean * along

    along3, flat3 = back_terms(scale3, inv3, mean3, shift3, slope_gain3, inv_w)

    def back_three(i, carry):
        at = block_at(i)
        m = mask[at, :]
        for j in range(wide_tiles):
            lanes = slice(LANES * j, LANES * (j + 1))
            g = gt[at, lanes] * scale3[:, lanes] - pre3[at, lanes] * along3[:, lanes] - m * flat3[:, lanes]
            gp3[at, lanes] = g.astype(BF16)
        return carry

    lax.fori_loop(0, blocks, back_three, 0)

    def back_expand(i, carry):
        at = pl.ds(pl.multiple_of(i * big, big), big)
        d = dot(gp3[at, :], wet[...]) * slope2[at, :]
        dz[at, :] = d
        return carry[0] + part_sum(d), carry[1] + part_sum(d * ((pre2[at, :] - mean2) * inv2))

    sums = lax.fori_loop(0, 2, back_expand, (zero_n, zero_n))
    send_sums(st5, 5, *sums)

    def grad_expand(i, carry):
        lanes = pl.ds(pl.multiple_of(i * 256, 256), 256)
        ge_ref[:, lanes] = dot(a2t[...], gp3[:, lanes]).astype(BF16)
        return carry

    lax.fori_loop(0, channels // 256, grad_expand, 0)
    if own_gather:
        cores(4).start()
        near(4)

    shift2, slope_gain2 = get_sums(st5, 5)
    along2, flat2 = back_terms(scale2, inv2, mean2, shift2, slope_gain2, inv_n)

    def back_two(i, carry):
        at = block_at(i)
        here = pl.ds(pl.multiple_of(i * BLOCK + pad, 8), BLOCK)
        m = both(mask[at, :])
        spad[1, here, :] = dz[at, :] * scale2 - m * (pre2[at, :] * along2 + flat2)
        return carry

    lax.fori_loop(0, blocks, back_two, 0)
    spread()
    gather_nine(True)

    def back_spatial(i, carry):
        at = pl.ds(pl.multiple_of(i * big, big), big)
        d = dot(nine[at, :], wst[...]) * slope1[at, :]
        dz[at, :] = d
        return carry[0] + part_sum(d), carry[1] + part_sum(d * ((pre1[at, :] - mean1) * inv1))

    sums = lax.fori_loop(0, 2, back_spatial, (zero_n, zero_n))
    send_sums(st6, 6, *sums)

    if own_gather:
        far(4)

    def grad_spatial(row):
        wide_row = 3 * narrow
        gs_refs[row][...] = dot(a1t[...], nine[:, wide_row * row : wide_row * (row + 1)]).astype(BF16)
        if own_gather:
            cores(1 + row).start()

    grad_spatial(0)
    grad_spatial(1)
    if own_gather:
        near(1)
    grad_spatial(2)
    if own_gather:
        near(2)
        near(3)

    shift1, slope_gain1 = get_sums(st6, 6)
    along1, flat1 = back_terms(scale1, inv1, mean1, shift1, slope_gain1, inv_n)

    def back_one(i, carry):
        at = block_at(i)
        g = dz[at, :] * scale1 - both(mask[at, :]) * (pre1[at, :] * along1 + flat1)
        gp1[at, :] = g.astype(BF16)
        return carry

    lax.fori_loop(0, blocks, back_one, 0)

    def grad_reduce(i, carry):
        lanes = pl.ds(pl.multiple_of(i * 256, 256), 256)
        gr_ref[lanes, :] = dot(xt[lanes, :], gp1[...]).astype(BF16)
        return carry

    lax.fori_loop(0, channels // 256, grad_reduce, 0)
    if own_gather:
        cores(0).start()
        far(1)
    pltpu.make_async_copy(os, os, out_sem.at[0]).wait()

    def grad_in(i, carry):
        at = pl.ds(pl.multiple_of(i * wide, wide), wide)
        m = mask[at, :]
        back = dot(gp1[at, :], wrt[...])
        for j in range(wide_tiles):
            lanes = slice(LANES * j, LANES * (j + 1))
            out_rows[j, at, :] = (m * back[:, lanes] + gt[at, lanes]).astype(BF16)
        return carry

    lax.fori_loop(0, rows // wide, grad_in, 0)
    if own_gather:
        near(0)
        far(2)
    from_rows().start()
    from_rows().wait()
    send_out(gin_hbm, 1)

    def own_part(ref, v):
        width = ref.shape[0]
        spot = frame * width
        tile = jnp.zeros((1, LANES), F32)
        for t in range(v.shape[1] // LANES):
            tile = jnp.where(lax.div(spot, LANES) == t, v[:, LANES * t : LANES * (t + 1)], tile)
        tile = pltpu.roll(jnp.concatenate([tile] * 8, axis=0), lax.rem(LANES - lax.rem(spot, LANES), LANES), 1)
        ref[...] = tile[0, 0:width]

    own_part(vec1_gain, slope_gain1)
    own_part(vec1_shift, shift1)
    own_part(vec2_gain, slope_gain2)
    own_part(vec2_shift, shift2)
    own_part(vec3_gain, slope_gain3)
    own_part(vec3_shift, shift3)

    if own_gather:
        owners(4)
        far(3)
        owners(1)
        far(0)
        for unit in (2, 3, 0):
            owners(unit)
        ge_out[...] = finished(4)[...].astype(F32)
        for row in range(3):
            fin = finished(1 + row)
            for c in range(3):
                gs_out[3 * row + c] = fin[:, narrow * c : narrow * (c + 1)].astype(F32)
        gr_out[...] = finished(0)[...].astype(F32)
    else:
        gr_out[...] = gr_ref[...]
        for row in range(3):
            gs_out[:, 3 * narrow * row : 3 * narrow * (row + 1)] = gs_refs[row][...]
        ge_out[...] = ge_ref[...]
    for index in range(3):
        weight_sent(index)
    pltpu.make_async_copy(os, os, out_sem.at[1]).wait()


def deliver_kernel(count, *refs):
    sources, targets, staged, sems = refs[:count], refs[count : 2 * count], refs[2 * count : 3 * count], refs[3 * count]
    pieces = []
    for i in range(count):
        cuts = 4 if sources[i].shape[0] % 16 == 0 and len(sources[i].shape) == 3 else 1
        size = sources[i].shape[0] // cuts
        for c in range(cuts):
            pieces.append((i, pl.ds(c * size, size), len(pieces)))
    into = [pltpu.make_async_copy(sources[i].at[at], staged[i].at[at], sems.at[0, k]) for i, at, k in pieces]
    away = [pltpu.make_async_copy(staged[i].at[at], targets[i].at[at], sems.at[1, k]) for i, at, k in pieces]
    for copy in into:
        copy.start()
    for arrive, leave in zip(into, away):
        arrive.wait()
        leave.start()
    for copy in away:
        copy.wait()


def deliver(arrays):
    return pl.pallas_call(
        functools.partial(deliver_kernel, len(arrays)),
        out_shape=tuple(jax.ShapeDtypeStruct(a.shape, a.dtype) for a in arrays),
        in_specs=[pl.BlockSpec(memory_space=pl.ANY)] * len(arrays),
        out_specs=(pl.BlockSpec(memory_space=pl.ANY),) * len(arrays),
        scratch_shapes=[pltpu.VMEM(a.shape, a.dtype) for a in arrays] + [pltpu.SemaphoreType.DMA((2, 64))],
    )(*arrays)


def on_device(
    dims,
    x_in,
    cotangent,
    w_reduce,
    w_spatial,
    w_expand,
    gain_one,
    shift_one,
    gain_two,
    shift_two,
    gain_three,
    shift_three,
    bucket,
    frame_count,
):
    clips, frames = dims
    slots, side, _, channels = x_in.shape
    narrow = w_reduce.shape[1]
    pixels = side * side
    rows = pixels * slots
    tiles = channels // LANES
    devices = clips * frames
    own_gather = all(n % 32 == 0 for n in (w_reduce.shape[0], w_spatial.shape[2], w_expand.shape[0]))
    w_spatial = w_spatial.reshape(9, -1, narrow)
    if not own_gather:
        w_reduce = lax.all_gather(w_reduce, "frame", axis=0, tiled=True)
        w_spatial = lax.all_gather(w_spatial, "frame", axis=1, tiled=True)
        w_expand = lax.all_gather(w_expand, "frame", axis=0, tiled=True)

    def by_pixel(v):
        return jnp.transpose(v, (1, 2, 0, 3)).reshape(pixels, slots, channels)

    any_spec = pl.BlockSpec(memory_space=pl.ANY)
    vmem = pl.BlockSpec(memory_space=pltpu.VMEM)
    smem = pl.BlockSpec(memory_space=pltpu.SMEM)
    big = jax.ShapeDtypeStruct((pixels, slots, channels), BF16)
    staged = pltpu.VMEM((tiles, pixels, slots, LANES), BF16)
    native = pltpu.VMEM((tiles, rows, LANES), BF16)
    narrow_f32 = pltpu.VMEM((rows, narrow), F32)
    wide_f32 = pltpu.VMEM((rows, channels), F32)
    lanes_f32 = pltpu.VMEM((rows, LANES), F32)

    def stats(count):
        return pltpu.VMEM((devices, count, LANES), F32)

    if own_gather:
        grad_shapes = (
            jax.ShapeDtypeStruct((channels // frames, narrow), F32),
            jax.ShapeDtypeStruct((9, narrow // frames, narrow), F32),
            jax.ShapeDtypeStruct((narrow // frames, channels), F32),
        )
    else:
        grad_shapes = (
            jax.ShapeDtypeStruct((channels, narrow), BF16),
            jax.ShapeDtypeStruct((narrow, 9 * narrow), BF16),
            jax.ShapeDtypeStruct((narrow, channels), BF16),
        )
    wholes = ((channels, narrow), *(((narrow, 3 * narrow),) * 3), (narrow, channels))
    lines = clips // 2
    unit_scratch = [pltpu.VMEM(shape, BF16) for shape in wholes]
    if own_gather:
        cuts = [(height // frames // 2, width) for height, width in wholes]
        unit_scratch += [pltpu.VMEM((frames, half, width), BF16) for half, width in cuts]
        unit_scratch += [
            pltpu.VMEM((frames // 2, half, width) if x_first else (frames, half, width // lines), BF16)
            for (half, width), x_first in zip(cuts, X_FIRST)
        ]
        unit_scratch += [pltpu.VMEM((frames, half, width // lines), BF16) for half, width in cuts]
        unit_scratch += [pltpu.VMEM((2 * half, width), BF16) for half, width in cuts]

    out, gin, gr, gs, ge, *vectors = pl.pallas_call(
        functools.partial(block_kernel, (clips, frames, side, own_gather)),
        out_shape=(
            big,
            big,
            *grad_shapes,
            *(jax.ShapeDtypeStruct((narrow // frames,), F32),) * 4,
            *(jax.ShapeDtypeStruct((channels // frames,), F32),) * 2,
        ),
        in_specs=[any_spec] * 5 + [vmem] * 6 + [smem] * 2,
        out_specs=(any_spec, any_spec) + (vmem,) * 9,
        scratch_shapes=[
            staged,
            staged,
            staged,
            native,
            native,
            native,
            pltpu.VMEM((rows, channels), BF16),
            pltpu.VMEM((channels, rows), BF16),
            pltpu.VMEM((narrow, rows), BF16),
            pltpu.VMEM((narrow, rows), BF16),
            lanes_f32,
            lanes_f32,
            lanes_f32,
            pltpu.VMEM((channels, narrow), BF16),
            pltpu.VMEM((9, narrow, narrow), BF16),
            pltpu.VMEM((narrow, channels), BF16),
            pltpu.VMEM((9 * narrow, narrow), BF16),
            pltpu.VMEM((channels, narrow), BF16),
            pltpu.VMEM((narrow, channels), BF16),
            narrow_f32,
            narrow_f32,
            narrow_f32,
            narrow_f32,
            narrow_f32,
            pltpu.VMEM((3, rows + 4 * side, narrow), F32),
            pltpu.VMEM((rows, narrow), BF16),
            pltpu.VMEM((rows, 9 * narrow), BF16),
            wide_f32,
            wide_f32,
            pltpu.VMEM((rows, channels), BF16),
            pltpu.VMEM((rows, narrow), BF16),
            pltpu.VMEM((frames, 8, LANES), F32),
            stats(1),
            stats(2 * narrow // LANES),
            stats(2 * narrow // LANES),
            stats(2 * tiles),
            stats(2 * tiles),
            stats(2 * narrow // LANES),
            stats(2 * narrow // LANES),
            pltpu.SemaphoreType.DMA((5,)),
            pltpu.SemaphoreType.DMA((3, 4, frames // 2)),
            pltpu.SemaphoreType.DMA((3, 4, frames // 2)),
            pltpu.SemaphoreType.DMA((8,)),
            pltpu.SemaphoreType.DMA((8,)),
            pltpu.SemaphoreType.DMA((3,)),
            pltpu.SemaphoreType.DMA((5, 4)),
            pltpu.SemaphoreType.DMA((5, 4)),
            *unit_scratch,
        ],
        compiler_params=pltpu.CompilerParams(
            collective_id=0, has_side_effects=True, vmem_limit_bytes=58 * 1024 * 1024
        ),
    )(
        by_pixel(x_in),
        by_pixel(cotangent),
        w_reduce,
        w_spatial,
        w_expand,
        gain_one,
        shift_one,
        gain_two,
        shift_two,
        gain_three,
        shift_three,
        bucket,
        frame_count,
    )

    def by_frame(v):
        return jnp.transpose(v.reshape(side, side, slots, channels), (2, 0, 1, 3))

    def owned(v):
        part = lax.psum_scatter(v, "frame", scatter_dimension=0, tiled=True)
        return lax.psum(part, "clip").astype(F32)

    if not own_gather:
        gr, gs, ge = owned(gr), owned(gs), owned(ge)
        gs = gs.reshape(-1, 9, narrow).transpose(1, 0, 2)
    out, gin, gr, gs, ge, *vectors = deliver((out, gin, gr, gs, ge, *vectors))
    return (by_frame(out), by_frame(gin), gr, gs.reshape(3, 3, -1, narrow), ge, *vectors)


def solution(mesh):
    by_device = P(("clip", "frame"))
    shard = P("frame")
    spatial = P(None, None, "frame", None)
    return jax.shard_map(
        functools.partial(on_device, (mesh.shape["clip"], mesh.shape["frame"])),
        mesh=mesh,
        in_specs=(by_device, by_device, shard, spatial) + (shard,) * 7 + (by_device, by_device),
        out_specs=(by_device, by_device, shard, spatial) + (shard,) * 7,
        check_vma=False,
    )
```

time: 126 us -> 93.5 us (0.74)
  Pallas kernels: 114 us -> 92 us
  local copies, waits for them, and re-layouts: 10.4 us -> 0 us
    pallas_call x1, Pallas kernels: 114 us -> 87.8 us  [on_device(): pl.pallas_call(functools.partial(block_kernel, (clips, frames, side, own_...]
    unnamed x31 -> x0, local copies, waits for them, and re-layouts: 10.4 us -> none
    pallas_call x0 -> x1, Pallas kernels: none -> 4.17 us  [deliver(): pl.pallas_call(functools.partial(deliver_kernel, len(arrays)), out_shape=...]
where the time goes in v2:
time: 93.5 us; the launch traced here: 93.3 us
  Pallas kernels  92 us (98%)
  between operations  1.3 us (1%)
    pallas_call x1, Pallas kernels, on_device(): pl.pallas_call(functools.partial(block_kernel, (clips, frames, side, own_...  87.8 us
    pallas_call x1, Pallas kernels, deliver(): pl.pallas_call(functools.partial(deliver_kernel, len(arrays)), out_shape=...  4.17 us

profile of v2, /device:TPU:0, one launch (start us, length us, event | category | flops | bytes accessed | tf_op | source)
XLA Modules:
  0.0 93.3 jit_solution(12504306162504589940)
XLA Ops:
  1.3 87.8 %shard_map.212 = (bf16[400,2,1024]{2,1,0:T(2,128)(2,1)}, bf16[400,2,1024]{2,1,0:T(2,128)(2,1)}, f32[128,256]{1,0:T(8,128)}, f32[9,32,256]{2,1,0:T(8,128)}, f32[3...) custom-call(bf16[400,2,1024]{2,1,0:T(2,128)(2,1)} %bitcast.14, ...), custom_call_target="tpu_custom_call" | custom-call | tf_op jit(solution)/shard_map/pallas_call | solution.py:882
  89.1 4.2 %shard_map.213 = (bf16[400,2,1024]{2,1,0:T(2,128)(2,1)}, bf16[400,2,1024]{2,1,0:T(2,128)(2,1)}, f32[128,256]{1,0:T(8,128)}, f32[9,32,256]{2,1,0:T(8,128)}, f32[3...) custom-call(bf16[400,2,1024]{2,1,0:T(2,128)(2,1)} %get-tuple-element, ...), custom_call_target="tpu_custom_call" | custom-call | tf_op jit(solution)/shard_map/pallas_call | solution.py:802

commit v3 on v2

--- a/solution.py
+++ b/solution.py
@@ -11,8 +11,9 @@
 EPS = 1e-05
 LANES = 128
 BLOCK = 80
+VMEM_BYTES = 52 * 1024 * 1024
 MESH = pl.DeviceIdType.MESH
-X_FIRST = (False, True, False, True, True)
+X_FIRST = (True, False, False, True, False, True)
 F32 = jnp.float32
 BF16 = jnp.bfloat16
 
@@ -49,8 +50,8 @@
     b3_ref,
     bucket_ref,
     count_ref,
-    out_hbm,
-    gin_hbm,
+    out_ref,
+    gin_ref,
     gr_out,
     gs_out,
     ge_out,
@@ -62,7 +63,6 @@
     vec3_shift,
     xs,
     cs,
-    os,
     x_rows,
     ct_rows,
     out_rows,
@@ -112,7 +112,7 @@
     clips, frames, side, own_gather = dims
     units = len(X_FIRST)
     full_refs, pair_refs, mid_refs, got_refs, fin_refs = [unit_refs[units * i : units * (i + 1)] for i in range(5)]
-    gr_ref, *gs_refs, ge_ref = full_refs
+    gr_refs, gs_refs, ge_ref = full_refs[0:2], full_refs[2:5], full_refs[5]
     devices = clips * frames
     clip = lax.axis_index("clip")
     frame = lax.axis_index("frame")
@@ -204,6 +204,14 @@
     edge = jnp.zeros((3, pad, narrow), F32)
     spad[:, 0:pad, :] = edge
     spad[:, pad + rows : 2 * pad + rows, :] = edge
+    turned = xm[...].T
+    if own_gather:
+        piece = part_r // 2
+        for f in range(2 * frames):
+            spot = (f % 2) * frames + f // 2
+            xt[piece * spot : piece * (spot + 1), :] = turned[piece * f : piece * (f + 1)]
+    else:
+        xt[...] = turned
     for copy in own_copies:
         copy.wait()
 
@@ -230,7 +238,7 @@
         most = buf.at[pl.ds(0, devices - 1)]
         pltpu.make_async_copy(most, most, st_recv.at[index]).wait()
         pltpu.make_async_copy(most, most, st_send.at[index]).wait()
-        return jnp.sum(buf[...], axis=0)
+        return jnp.sum(buf[...].astype(F32), axis=0)
 
     across = lax.rem(frame, 2)
     along = lax.div(frame, 2)
@@ -327,6 +335,8 @@
     for d in range(1, depth):
         along_x(0, d)
         to_core(0, d)
+    along_x(1, 1)
+    to_core(1, 1)
     for d in range(depth):
         to_core_late(0, d)
 
@@ -461,15 +471,13 @@
 
     sums = lax.fori_loop(0, 2, conv_one, (zero_n, zero_n))
     send_sums(st1, 1, *sums)
-    for d in range(1, depth):
+    for d in range(2, depth):
         along_x(1, d)
         to_core(1, d)
     along_z(2)
     along_x(2, 0)
     for d in range(depth):
         to_core_late(1, d)
-    xt[...] = xm[...].T
-
     most = par.at[pl.ds(0, frames - 1)]
     pltpu.make_async_copy(most, most, st_recv.at[0]).wait()
     pltpu.make_async_copy(most, most, st_send.at[0]).wait()
@@ -562,25 +570,28 @@
         z = pre2[at, :] * scale2 + offset2
         s = sigmoid(z)
         ms = both(mask[at, :]) * s
-        act2[at, :] = (ms * z).astype(BF16)
+        a = (ms * z).astype(BF16)
+        act2[at, :] = a
         slope2[at, :] = ms * (1.0 + z * (1.0 - s))
-        return carry
-
-    lax.fori_loop(0, blocks, act_two, 0)
+        return carry + part_sum(a.astype(F32))
+
+    act_sum = lax.fori_loop(0, blocks, act_two, zero_n)
 
     weight_ready(2)
     zero_w = jnp.zeros((8, channels), F32)
 
-    wide = 2 * BLOCK
+    wide = big
 
     def conv_three(i, carry):
         at = pl.ds(pl.multiple_of(i * wide, wide), wide)
         v = dot(act2[at, :], we[...])
         pre3[at, :] = v
-        return carry[0] + part_sum(v), carry[1] + part_sum(v * v)
-
-    sums = lax.fori_loop(0, rows // wide, conv_three, (zero_w, zero_w))
-    send_sums(st3, 3, *sums)
+        return carry + part_sum(v * v)
+
+    squares = lax.fori_loop(0, rows // wide, conv_three, zero_w)
+    st3[me, :, 0:narrow] = jnp.sum(act_sum, axis=0, keepdims=True)
+    st3[me, :, narrow : narrow + channels] = jnp.sum(squares, axis=0, keepdims=True)
+    gather_to_all(st3, 3)
     for tap in range(9):
         wst[narrow * tap : narrow * (tap + 1), :] = ws[tap].T
     wet[...] = we[...].T
@@ -588,17 +599,20 @@
     copies_in(cs, 1).wait()
     to_rows(cs, ct_rows, 1).start()
     to_rows(cs, ct_rows, 1).wait()
-    mean3, inv3 = moments(st3, 3, inv_w)
+    both_sums = arrived(st3, 3)
+    left = both_sums[:, 0:narrow]
+    parts = []
+    for _ in range(3):
+        parts.append(left.astype(BF16).astype(F32))
+        left = left - parts[-1]
+    exact = jnp.concatenate(parts + [jnp.zeros((5, narrow), F32)], axis=0).astype(BF16)
+    mean3 = jnp.sum(dot(exact, we[...]), axis=0, keepdims=True) * inv_w
+    inv3 = lax.rsqrt(both_sums[:, narrow:] * inv_w - mean3 * mean3 + EPS)
     scale3 = inv3 * gain3
     offset3 = bias3 - mean3 * scale3
 
-    def from_rows():
-        return pltpu.make_async_copy(out_rows, os.reshape(wide_tiles, rows, LANES), out_sem.at[2])
-
-    def send_out(ref, index):
-        for j in range(wide_tiles):
-            lanes = pl.ds(LANES * j, LANES)
-            pltpu.make_async_copy(os.at[j], ref.at[:, :, lanes], out_sem.at[index]).start()
+    def from_rows(ref, index):
+        return pltpu.make_async_copy(out_rows, ref.reshape(wide_tiles, rows, LANES), out_sem.at[index])
 
     def finish(i, carry):
         at = block_at(i)
@@ -610,18 +624,21 @@
             t = p * scale3[:, lanes] + offset3[:, lanes] + xm[at, lanes].astype(F32)
             s = sigmoid(t)
             ms = m * s
-            out_rows[j, at, :] = (ms * t).astype(BF16)
-            g = ct_rows[j, at, :].astype(F32) * (ms * (1.0 + t * (1.0 - s)))
+            o = ms * t
+            out_rows[j, at, :] = o.astype(BF16)
+            g = ct_rows[j, at, :].astype(F32) * (ms + o * (1.0 - s))
             gt[at, lanes] = g
             first.append(part_sum(g))
-            second.append(part_sum(g * ((p - mean3[:, lanes]) * inv3[:, lanes])))
+            second.append(part_sum(g * p))
         return carry[0] + jnp.concatenate(first, axis=1), carry[1] + jnp.concatenate(second, axis=1)
 
-    sums = lax.fori_loop(0, blocks, finish, (zero_w, zero_w))
-    send_sums(st4, 4, *sums)
-    from_rows().start()
-    from_rows().wait()
-    send_out(out_hbm, 0)
+    shift_own, slope_own = lax.fori_loop(0, blocks, finish, (zero_w, zero_w))
+    shift_own = jnp.sum(shift_own, axis=0, keepdims=True)
+    slope_own = (jnp.sum(slope_own, axis=0, keepdims=True) - mean3 * shift_own) * inv3
+    pieces = [v[:, LANES * j : LANES * (j + 1)] for v in (shift_own, slope_own) for j in range(wide_tiles)]
+    st4[me] = jnp.concatenate(pieces, axis=0).astype(BF16)
+    gather_to_all(st4, 4)
+    from_rows(out_ref, 0).start()
     shift3, slope_gain3 = get_sums(st4, 4)
 
     def back_terms(scale, inv, mean, shift_sum, gain_sum, inv_cnt):
@@ -641,14 +658,9 @@
 
     lax.fori_loop(0, blocks, back_three, 0)
 
-    def back_expand(i, carry):
-        at = pl.ds(pl.multiple_of(i * big, big), big)
-        d = dot(gp3[at, :], wet[...]) * slope2[at, :]
-        dz[at, :] = d
-        return carry[0] + part_sum(d), carry[1] + part_sum(d * ((pre2[at, :] - mean2) * inv2))
-
-    sums = lax.fori_loop(0, 2, back_expand, (zero_n, zero_n))
-    send_sums(st5, 5, *sums)
+    d = dot(gp3[...], wet[...]) * slope2[...]
+    dz[...] = d
+    send_sums(st5, 5, part_sum(d), part_sum(d * ((pre2[...] - mean2) * inv2)))
 
     def grad_expand(i, carry):
         lanes = pl.ds(pl.multiple_of(i * 256, 256), 256)
@@ -657,8 +669,8 @@
 
     lax.fori_loop(0, channels // 256, grad_expand, 0)
     if own_gather:
-        cores(4).start()
-        near(4)
+        cores(5).start()
+        near(5)
 
     shift2, slope_gain2 = get_sums(st5, 5)
     along2, flat2 = back_terms(scale2, inv2, mean2, shift2, slope_gain2, inv_n)
@@ -674,6 +686,14 @@
     spread()
     gather_nine(True)
 
+    def grad_spatial(row):
+        wide_row = 3 * narrow
+        gs_refs[row][...] = dot(a1t[...], nine[:, wide_row * row : wide_row * (row + 1)]).astype(BF16)
+        if own_gather:
+            cores(2 + row).start()
+
+    grad_spatial(0)
+
     def back_spatial(i, carry):
         at = pl.ds(pl.multiple_of(i * big, big), big)
         d = dot(nine[at, :], wst[...]) * slope1[at, :]
@@ -682,24 +702,14 @@
 
     sums = lax.fori_loop(0, 2, back_spatial, (zero_n, zero_n))
     send_sums(st6, 6, *sums)
-
-    if own_gather:
-        far(4)
-
-    def grad_spatial(row):
-        wide_row = 3 * narrow
-        gs_refs[row][...] = dot(a1t[...], nine[:, wide_row * row : wide_row * (row + 1)]).astype(BF16)
-        if own_gather:
-            cores(1 + row).start()
-
-    grad_spatial(0)
+    if own_gather:
+        near(2)
+        far(5)
     grad_spatial(1)
-    if own_gather:
-        near(1)
     grad_spatial(2)
     if own_gather:
-        near(2)
         near(3)
+        near(4)
 
     shift1, slope_gain1 = get_sums(st6, 6)
     along1, flat1 = back_terms(scale1, inv1, mean1, shift1, slope_gain1, inv_n)
@@ -712,16 +722,16 @@
 
     lax.fori_loop(0, blocks, back_one, 0)
 
-    def grad_reduce(i, carry):
-        lanes = pl.ds(pl.multiple_of(i * 256, 256), 256)
-        gr_ref[lanes, :] = dot(xt[lanes, :], gp1[...]).astype(BF16)
-        return carry
-
-    lax.fori_loop(0, channels // 256, grad_reduce, 0)
-    if own_gather:
-        cores(0).start()
-        far(1)
-    pltpu.make_async_copy(os, os, out_sem.at[0]).wait()
+    for i in range(2):
+        height = channels // 2
+        gr_refs[i][...] = dot(xt[height * i : height * (i + 1), :], gp1[...]).astype(BF16)
+        if own_gather:
+            cores(i).start()
+    if own_gather:
+        far(2)
+        near(0)
+        near(1)
+    from_rows(out_ref, 0).wait()
 
     def grad_in(i, carry):
         at = pl.ds(pl.multiple_of(i * wide, wide), wide)
@@ -734,11 +744,9 @@
 
     lax.fori_loop(0, rows // wide, grad_in, 0)
     if own_gather:
-        near(0)
-        far(2)
-    from_rows().start()
-    from_rows().wait()
-    send_out(gin_hbm, 1)
+        far(3)
+        far(4)
+    from_rows(gin_ref, 1).start()
 
     def own_part(ref, v):
         width = ref.shape[0]
@@ -757,54 +765,54 @@
     own_part(vec3_shift, shift3)
 
     if own_gather:
-        owners(4)
-        far(3)
-        owners(1)
+        owners(5)
         far(0)
-        for unit in (2, 3, 0):
+        far(1)
+        for unit in (2, 3, 4, 0, 1):
             owners(unit)
-        ge_out[...] = finished(4)[...].astype(F32)
+        ge_out[...] = finished(5)[...].astype(F32)
         for row in range(3):
-            fin = finished(1 + row)
+            fin = finished(2 + row)
             for c in range(3):
                 gs_out[3 * row + c] = fin[:, narrow * c : narrow * (c + 1)].astype(F32)
-        gr_out[...] = finished(0)[...].astype(F32)
+        for i in range(2):
+            gr_out[piece * i : piece * (i + 1), :] = finished(i)[...].astype(F32)
     else:
-        gr_out[...] = gr_ref[...]
+        for i in range(2):
+            gr_out[channels // 2 * i : channels // 2 * (i + 1), :] = gr_refs[i][...]
         for row in range(3):
             gs_out[:, 3 * narrow * row : 3 * narrow * (row + 1)] = gs_refs[row][...]
         ge_out[...] = ge_ref[...]
     for index in range(3):
         weight_sent(index)
-    pltpu.make_async_copy(os, os, out_sem.at[1]).wait()
+    from_rows(gin_ref, 1).wait()
 
 
 def deliver_kernel(count, *refs):
-    sources, targets, staged, sems = refs[:count], refs[count : 2 * count], refs[2 * count : 3 * count], refs[3 * count]
-    pieces = []
-    for i in range(count):
-        cuts = 4 if sources[i].shape[0] % 16 == 0 and len(sources[i].shape) == 3 else 1
-        size = sources[i].shape[0] // cuts
-        for c in range(cuts):
-            pieces.append((i, pl.ds(c * size, size), len(pieces)))
-    into = [pltpu.make_async_copy(sources[i].at[at], staged[i].at[at], sems.at[0, k]) for i, at, k in pieces]
-    away = [pltpu.make_async_copy(staged[i].at[at], targets[i].at[at], sems.at[1, k]) for i, at, k in pieces]
-    for copy in into:
+    sources, targets, sems = refs[:count], refs[count : 2 * count], refs[2 * count]
+    copies = []
+    for i in range(2):
+        for j in range(sources[i].shape[0]):
+            part = targets[i].at[:, :, LANES * j : LANES * (j + 1)]
+            copies.append(pltpu.make_async_copy(sources[i].at[j], part, sems.at[len(copies)]))
+    for i in range(2, count):
+        copies.append(pltpu.make_async_copy(sources[i], targets[i], sems.at[len(copies)]))
+    for copy in copies:
         copy.start()
-    for arrive, leave in zip(into, away):
-        arrive.wait()
-        leave.start()
-    for copy in away:
+    for copy in copies:
         copy.wait()
 
 
-def deliver(arrays):
+def deliver(arrays, big):
+    count = len(arrays)
+    shapes = [big, big] + [jax.ShapeDtypeStruct(a.shape, a.dtype) for a in arrays[2:]]
     return pl.pallas_call(
-        functools.partial(deliver_kernel, len(arrays)),
-        out_shape=tuple(jax.ShapeDtypeStruct(a.shape, a.dtype) for a in arrays),
-        in_specs=[pl.BlockSpec(memory_space=pl.ANY)] * len(arrays),
-        out_specs=(pl.BlockSpec(memory_space=pl.ANY),) * len(arrays),
-        scratch_shapes=[pltpu.VMEM(a.shape, a.dtype) for a in arrays] + [pltpu.SemaphoreType.DMA((2, 64))],
+        functools.partial(deliver_kernel, count),
+        out_shape=tuple(shapes),
+        in_specs=[pl.BlockSpec(memory_space=pltpu.VMEM)] * count,
+        out_specs=(pl.BlockSpec(memory_space=pl.ANY),) * count,
+        scratch_shapes=[pltpu.SemaphoreType.DMA((2 * arrays[0].shape[0] + count,))],
+        compiler_params=pltpu.CompilerParams(vmem_limit_bytes=1024 * 1024),
     )(*arrays)
 
 
@@ -856,9 +864,9 @@
 
     if own_gather:
         grad_shapes = (
-            jax.ShapeDtypeStruct((channels // frames, narrow), F32),
-            jax.ShapeDtypeStruct((9, narrow // frames, narrow), F32),
-            jax.ShapeDtypeStruct((narrow // frames, channels), F32),
+            pltpu.VMEM((channels // frames, narrow), F32),
+            pltpu.VMEM((9, narrow // frames, narrow), F32),
+            pltpu.VMEM((narrow // frames, channels), F32),
         )
     else:
         grad_shapes = (
@@ -866,7 +874,7 @@
             jax.ShapeDtypeStruct((narrow, 9 * narrow), BF16),
             jax.ShapeDtypeStruct((narrow, channels), BF16),
         )
-    wholes = ((channels, narrow), *(((narrow, 3 * narrow),) * 3), (narrow, channels))
+    wholes = (*(((channels // 2, narrow),) * 2), *(((narrow, 3 * narrow),) * 3), (narrow, channels))
     lines = clips // 2
     unit_scratch = [pltpu.VMEM(shape, BF16) for shape in wholes]
     if own_gather:
@@ -879,19 +887,18 @@
         unit_scratch += [pltpu.VMEM((frames, half, width // lines), BF16) for half, width in cuts]
         unit_scratch += [pltpu.VMEM((2 * half, width), BF16) for half, width in cuts]
 
-    out, gin, gr, gs, ge, *vectors = pl.pallas_call(
+    results = pl.pallas_call(
         functools.partial(block_kernel, (clips, frames, side, own_gather)),
         out_shape=(
-            big,
-            big,
+            staged,
+            staged,
             *grad_shapes,
-            *(jax.ShapeDtypeStruct((narrow // frames,), F32),) * 4,
-            *(jax.ShapeDtypeStruct((channels // frames,), F32),) * 2,
+            *(pltpu.VMEM((narrow // frames,), F32),) * 4,
+            *(pltpu.VMEM((channels // frames,), F32),) * 2,
         ),
         in_specs=[any_spec] * 5 + [vmem] * 6 + [smem] * 2,
-        out_specs=(any_spec, any_spec) + (vmem,) * 9,
+        out_specs=(vmem,) * 11,
         scratch_shapes=[
-            staged,
             staged,
             staged,
             native,
@@ -926,8 +933,8 @@
             stats(1),
             stats(2 * narrow // LANES),
             stats(2 * narrow // LANES),
-            stats(2 * tiles),
-            stats(2 * tiles),
+            pltpu.VMEM((devices, 1, narrow + channels), F32),
+            pltpu.VMEM((devices, 2 * tiles, LANES), BF16),
             stats(2 * narrow // LANES),
             stats(2 * narrow // LANES),
             pltpu.SemaphoreType.DMA((5,)),
@@ -935,13 +942,13 @@
             pltpu.SemaphoreType.DMA((3, 4, frames // 2)),
             pltpu.SemaphoreType.DMA((8,)),
             pltpu.SemaphoreType.DMA((8,)),
-            pltpu.SemaphoreType.DMA((3,)),
-            pltpu.SemaphoreType.DMA((5, 4)),
-            pltpu.SemaphoreType.DMA((5, 4)),
+            pltpu.SemaphoreType.DMA((2,)),
+            pltpu.SemaphoreType.DMA((len(X_FIRST), 4)),
+            pltpu.SemaphoreType.DMA((len(X_FIRST), 4)),
             *unit_scratch,
         ],
         compiler_params=pltpu.CompilerParams(
-            collective_id=0, has_side_effects=True, vmem_limit_bytes=58 * 1024 * 1024
+            collective_id=0, has_side_effects=True, vmem_limit_bytes=VMEM_BYTES
         ),
     )(
         by_pixel(x_in),
@@ -966,10 +973,12 @@
         part = lax.psum_scatter(v, "frame", scatter_dimension=0, tiled=True)
         return lax.psum(part, "clip").astype(F32)
 
-    if not own_gather:
-        gr, gs, ge = owned(gr), owned(gs), owned(ge)
+    if own_gather:
+        out, gin, gr, gs, ge, *vectors = deliver(results, big)
+    else:
+        gr, gs, ge = [owned(v) for v in results[2:5]]
         gs = gs.reshape(-1, 9, narrow).transpose(1, 0, 2)
-    out, gin, gr, gs, ge, *vectors = deliver((out, gin, gr, gs, ge, *vectors))
+        out, gin, gr, gs, ge, *vectors = deliver((*results[:2], gr, gs, ge, *results[5:]), big)
     return (by_frame(out), by_frame(gin), gr, gs.reshape(3, 3, -1, narrow), ge, *vectors)
 
 

time: 93.5 us -> 83.6 us (0.89)
  Pallas kernels: 92 us -> 82.1 us
    pallas_call x1, Pallas kernels: 87.8 us -> 80 us  [on_device(): pl.pallas_call(functools.partial(block_kernel, (clips, frames, side, own_...]
    pallas_call x1, Pallas kernels: 4.17 us -> 2.14 us  [deliver(): pl.pallas_call(functools.partial(deliver_kernel, count), out_shape=tuple(...]
where the time goes in v3:
time: 83.6 us; the launch traced here: 83.5 us
  Pallas kernels  82.1 us (98%)
  between operations  1.3 us (2%)
    pallas_call x1, Pallas kernels, on_device(): pl.pallas_call(functools.partial(block_kernel, (clips, frames, side, own_...  80 us
    pallas_call x1, Pallas kernels, deliver(): pl.pallas_call(functools.partial(deliver_kernel, count), out_shape=tuple(...  2.14 us

profile of v3, /device:TPU:0, one launch (start us, length us, event | category | flops | bytes accessed | tf_op | source)
XLA Modules:
  0.0 83.5 jit_solution(14148785295902718666)
XLA Ops:
  1.3 80.0 %shard_map.212 = (bf16[8,400,2,128]{3,2,1,0:T(2,128)(2,1)S(1)}, bf16[8,400,2,128]{3,2,1,0:T(2,128)(2,1)S(1)}, f32[128,256]{1,0:T(8,128)S(1)}, f32[9,32,256]{2,1,...) custom-call(bf16[400,2,1024]{2,1,0:T(2,128)(2,1)} %bitcast.14, ...), custom_call_target="tpu_custom_call" | custom-call | tf_op jit(solution)/shard_map/pallas_call | solution.py:890
  81.3 2.1 %shard_map.213 = (bf16[400,2,1024]{2,1,0:T(2,128)(2,1)}, bf16[400,2,1024]{2,1,0:T(2,128)(2,1)}, f32[128,256]{1,0:T(8,128)}, f32[9,32,256]{2,1,0:T(8,128)}, f32[3...) custom-call(bf16[8,400,2,128]{3,2,1,0:T(2,128)(2,1)S(1)} %get-tuple-, ...), custom_call_target="tpu_custom_call" | custom-call | tf_op jit(solution)/shard_map/pallas_call | solution.py:809

commit v4 on v3

--- a/solution.py
+++ b/solution.py
@@ -13,7 +13,7 @@
 BLOCK = 80
 VMEM_BYTES = 52 * 1024 * 1024
 MESH = pl.DeviceIdType.MESH
-X_FIRST = (True, False, False, True, False, True)
+NEAR = ("x", "y", "y", "x", "y", "x")
 F32 = jnp.float32
 BF16 = jnp.bfloat16
 
@@ -110,7 +110,7 @@
     *unit_refs,
 ):
     clips, frames, side, own_gather = dims
-    units = len(X_FIRST)
+    units = len(NEAR)
     full_refs, pair_refs, mid_refs, got_refs, fin_refs = [unit_refs[units * i : units * (i + 1)] for i in range(5)]
     gr_refs, gs_refs, ge_ref = full_refs[0:2], full_refs[2:5], full_refs[5]
     devices = clips * frames
@@ -126,9 +126,33 @@
     nar_tiles = narrow // LANES
     blocks = rows // BLOCK
     pad = 2 * side
-
-    def other(k):
-        return (lax.rem(clip + lax.div(k, frames), clips), lax.rem(frame + lax.rem(k, frames), frames))
+    lines = clips // 2
+    line_me = lax.div(clip, 2)
+    y_peer = (lax.rem(clip + 2, clips), frame)
+
+    small = devices <= 32 and clips & (clips - 1) == 0 and frames & (frames - 1) == 0
+
+    def flips(v, size):
+        return [(1 - 2 * lax.rem(lax.div(v, 1 << i), 2)) * (1 << i) for i in range(size.bit_length() - 1)]
+
+    clip_flips, frame_flips = flips(clip, clips), flips(frame, frames)
+
+    def to_others(action):
+        if small:
+            for b in reversed(range(frames)):
+                to_frame = sum((d for i, d in enumerate(frame_flips) if b >> i & 1), frame)
+                for a in reversed(range(clips)):
+                    if a or b:
+                        action((sum((d for i, d in enumerate(clip_flips) if a >> i & 1), clip), to_frame))
+            return
+        for a in range(clips):
+            to_clip = lax.rem(clip + a, clips)
+
+            def step(b, carry):
+                action((to_clip, lax.rem(frame + b, frames)))
+                return carry
+
+            lax.fori_loop(0 if a else 1, frames, step, 0)
 
     for j in range(wide_tiles):
         lanes = pl.ds(LANES * j, LANES)
@@ -161,11 +185,7 @@
 
     barrier = pltpu.get_barrier_semaphore()
 
-    def greet(k, carry):
-        pl.semaphore_signal(barrier, inc=1, device_id=other(k), device_id_type=MESH)
-        return carry
-
-    lax.fori_loop(1, devices, greet, 0)
+    to_others(lambda target: pl.semaphore_signal(barrier, inc=1, device_id=target, device_id_type=MESH))
 
     row_id = lax.broadcasted_iota(jnp.int32, (rows, LANES), 0)
     pixel = row_id >> 1
@@ -218,26 +238,21 @@
     pl.semaphore_wait(barrier, devices - 1)
 
     def gather_to_all(buf, index):
-        for a in range(clips):
-            to_clip = lax.rem(clip + a, clips)
-
-            def send(b, carry):
-                pltpu.make_async_remote_copy(
-                    src_ref=buf.at[me],
-                    dst_ref=buf.at[me],
-                    send_sem=st_send.at[index],
-                    recv_sem=st_recv.at[index],
-                    device_id=(to_clip, lax.rem(frame + b, frames)),
-                    device_id_type=MESH,
-                ).start()
-                return carry
-
-            lax.fori_loop(0 if a else 1, frames, send, 0)
+        def send(target):
+            pltpu.make_async_remote_copy(
+                src_ref=buf.at[me],
+                dst_ref=buf.at[me],
+                send_sem=st_send.at[0],
+                recv_sem=st_recv.at[index],
+                device_id=target,
+                device_id_type=MESH,
+            ).start()
+
+        to_others(send)
 
     def arrived(buf, index):
         most = buf.at[pl.ds(0, devices - 1)]
         pltpu.make_async_copy(most, most, st_recv.at[index]).wait()
-        pltpu.make_async_copy(most, most, st_send.at[index]).wait()
         return jnp.sum(buf[...].astype(F32), axis=0)
 
     across = lax.rem(frame, 2)
@@ -250,74 +265,97 @@
 
     if own_gather:
 
-        def halves(ref, axis, part):
-            half = part // 2
-
-            def view(owner):
-                at = pl.ds(pl.multiple_of(owner * part + core * half, half), half)
-                return ref.at[at] if axis == 0 else ref.at[:, at]
-
-            return view
-
-        views = (halves(wr, 0, part_r), halves(ws, 1, part_s), halves(we, 0, part_e))
-
-        def weight_copy(index, hop, d, owner, target):
-            part = views[index](owner)
+        kinds = ((wr, 0, part_r), (ws, 1, part_s), (we, 0, part_e))
+
+        def piece_of(index, owner, columns=None):
+            ref, axis, part = kinds[index]
+            at = pl.ds(pl.multiple_of(owner * part + core * (part // 2), part // 2), part // 2)
+            if axis == 0:
+                return ref.at[at]
+            return ref.at[:, at] if columns is None else ref.at[:, at, columns]
+
+        def own_columns(index):
+            if index != 1:
+                return None
+            cut = narrow // lines
+            return pl.ds(pl.multiple_of(line_me * cut, LANES), cut)
+
+        def weight_copy(index, sem, owner, target, columns=None):
+            part = piece_of(index, owner, columns)
             return pltpu.make_async_remote_copy(
                 src_ref=part,
                 dst_ref=part,
-                send_sem=wsend.at[index, hop, d],
-                recv_sem=wrecv.at[index, hop, d],
+                send_sem=wsend.at[index],
+                recv_sem=wrecv.at[index, sem],
                 device_id=target,
                 device_id_type=MESH,
             )
 
+        def blocks_of(index, count, wide=True):
+            ref, axis, part = kinds[index]
+            size = pl.ds(0, count * (part // 2))
+            if axis == 0:
+                return ref.at[size]
+            return ref.at[:, size] if wide else ref.at[:, size, pl.ds(0, narrow // lines)]
+
+        def blocks_wait(sem, view):
+            pltpu.make_async_copy(view, view, sem).wait()
+
         def along_z(index):
             for d in range(1, depth):
                 target = (clip, lax.rem(along + d, depth) * 2 + across)
-                weight_copy(index, 0, d, frame, target).start()
+                weight_copy(index, d, frame, target, own_columns(index)).start()
 
         def along_x(index, d):
+            columns = own_columns(index)
             if d:
-                weight_copy(index, 0, d, owner_at(d, across), x_peer).wait_recv()
-            weight_copy(index, 1, d, owner_at(d, across), x_peer).start()
+                weight_copy(index, d, owner_at(d, across), x_peer, columns).wait_recv()
+            weight_copy(index, depth + d, owner_at(d, across), x_peer, columns).start()
+
+        def along_y(d):
+            weight_copy(1, 2 * depth + 1, owner_at(d, across), y_peer, own_columns(1)).start()
+
+        def along_y_late(d):
+            owner = owner_at(d, 1 - across)
+            weight_copy(1, depth + d, owner, partner, own_columns(1)).wait_recv()
+            weight_copy(1, 2 * depth + 2, owner, y_peer, own_columns(1)).start()
+
+        def y_to_core():
+            blocks_wait(wrecv.at[1, 2 * depth + 1], blocks_of(1, depth - 1, False))
+            for d in range(1, depth):
+                to_core(1, d)
+            blocks_wait(wrecv.at[1, 2 * depth + 2], blocks_of(1, depth, False))
+            for d in range(depth):
+                weight_copy(1, 2 * depth, owner_at(d, 1 - across), partner).start()
 
         def to_core(index, d):
-            if d:
-                weight_copy(index, 2, d, owner_at(d, across), partner).start()
+            weight_copy(index, 2 * depth, owner_at(d, across), partner).start()
 
         def to_core_late(index, d):
             owner = owner_at(d, 1 - across)
-            weight_copy(index, 1, d, owner, partner).wait_recv()
-            weight_copy(index, 3, d, owner, partner).start()
+            weight_copy(index, depth + d, owner, partner).wait_recv()
+            weight_copy(index, 2 * depth, owner, partner).start()
 
         def weight_ready(index):
-            for d in range(depth):
-                if d:
-                    weight_copy(index, 2, d, owner_at(d, across), partner).wait_recv()
-                weight_copy(index, 3, d, owner_at(d, 1 - across), partner).wait_recv()
+            blocks_wait(wrecv.at[index, 2 * depth], blocks_of(index, 2 * depth - 1))
 
         def weight_sent(index):
-            for d in range(depth):
-                if d:
-                    weight_copy(index, 0, d, frame, partner).wait_send()
-                    weight_copy(index, 2, d, frame, partner).wait_send()
-                weight_copy(index, 1, d, frame, partner).wait_send()
-                weight_copy(index, 3, d, frame, partner).wait_send()
+            blocks_wait(wsend.at[index], blocks_of(index, 4 * depth - 2))
 
     else:
 
         def nothing(*args):
             pass
 
-        along_z = along_x = to_core = to_core_late = weight_ready = weight_sent = nothing
+        along_z = along_x = along_y = along_y_late = y_to_core = nothing
+        to_core = to_core_late = weight_ready = weight_sent = nothing
 
     def send_params():
         def send(b, carry):
             pltpu.make_async_remote_copy(
                 src_ref=par.at[frame],
                 dst_ref=par.at[frame],
-                send_sem=st_send.at[0],
+                send_sem=st_send.at[1],
                 recv_sem=st_recv.at[0],
                 device_id=(clip, lax.rem(frame + b, frames)),
                 device_id_type=MESH,
@@ -336,7 +374,7 @@
         along_x(0, d)
         to_core(0, d)
     along_x(1, 1)
-    to_core(1, 1)
+    along_y(1)
     for d in range(depth):
         to_core_late(0, d)
 
@@ -364,16 +402,12 @@
 
     zero_n = jnp.zeros((8, narrow), F32)
 
-    lines = clips // 2
-    line_me = lax.div(clip, 2)
-    peers = frames
-    y_peer = (lax.rem(clip + 2, clips), frame)
 
     def unit_copy(unit, stage, src, dst, target):
         return pltpu.make_async_remote_copy(
             src_ref=src,
             dst_ref=dst,
-            send_sem=rs_send.at[unit, stage],
+            send_sem=rs_send.at[unit],
             recv_sem=rs_recv.at[unit, stage],
             device_id=target,
             device_id_type=MESH,
@@ -392,13 +426,13 @@
     def near_copy(unit):
         pair, mid = pair_refs[unit], mid_refs[unit]
         half, width = pair.shape[1], pair.shape[2]
-        if X_FIRST[unit]:
+        if NEAR[unit] == "x":
             return unit_copy(unit, 1, pair.reshape(depth, 2, half, width).at[:, 1 - across], mid, x_peer)
         return unit_copy(unit, 1, pair.at[:, :, columns(1 - line_me, width // lines)], mid, y_peer)
 
     def near(unit):
         full, pair = full_refs[unit], pair_refs[unit]
-        cores(unit).wait()
+        cores(unit).wait_recv()
         half = pair.shape[1]
         mine = pl.ds(pl.multiple_of(core * half, half), half)
         view = full.reshape(frames, 2 * half, full.shape[1])
@@ -408,20 +442,34 @@
             return carry
 
         lax.fori_loop(0, frames, add, 0)
-        near_copy(unit).start()
+        if NEAR[unit]:
+            near_copy(unit).start()
 
     def far(unit):
         pair, mid, got = pair_refs[unit], mid_refs[unit], got_refs[unit]
         cut = pair.shape[2] // lines
-        near_copy(unit).wait()
+        if NEAR[unit]:
+            near_copy(unit).wait_recv()
 
         def add(k, carry):
-            own = pair[2 * k + across] if X_FIRST[unit] else pair[k, :, columns(line_me, cut)]
+            own = pair[2 * k + across] if NEAR[unit] == "x" else pair[k, :, columns(line_me, cut)]
             mid[k] = (mid[k].astype(F32) + own.astype(F32)).astype(BF16)
             return carry
 
-        lax.fori_loop(0, mid.shape[0], add, 0)
-        if X_FIRST[unit]:
+        if NEAR[unit]:
+            lax.fori_loop(0, mid.shape[0], add, 0)
+        if not NEAR[unit]:
+            slot_me = line_me * frames + frame
+            got[slot_me] = pair[frame, :, columns(line_me, cut)]
+
+            def send(k, carry):
+                line = lax.rem(line_me + lax.div(k, frames), lines)
+                owner = lax.rem(frame + lax.rem(k, frames), frames)
+                src = pair.at[owner, :, columns(line, cut)]
+                unit_copy(unit, 2, src, got.at[slot_me], (line * 2 + core, owner)).start()
+                return carry
+
+        elif NEAR[unit] == "x":
             slot_me = line_me * depth + along
             got[slot_me] = mid[along, :, columns(line_me, cut)]
 
@@ -440,13 +488,13 @@
                 unit_copy(unit, 2, mid.at[owner], got.at[frame], (clip, owner)).start()
                 return carry
 
-        lax.fori_loop(1, peers, send, 0)
+        lax.fori_loop(1, got.shape[0], send, 0)
 
     def owners(unit):
         got, fin = got_refs[unit], fin_refs[unit]
         half, cut = got.shape[1], got.shape[2]
-        most = got.at[pl.ds(0, peers - 1)]
-        unit_copy(unit, 2, most, most, partner).wait()
+        most = got.at[pl.ds(0, got.shape[0] - 1)]
+        unit_copy(unit, 2, most, most, partner).wait_recv()
         spot = fin.at[pl.ds(pl.multiple_of(core * half, half), half), columns(line_me, cut)]
         spot[...] = jnp.sum(got[...].astype(F32), axis=0).astype(BF16)
 
@@ -458,8 +506,17 @@
 
     def finished(unit):
         most = got_refs[unit].at[pl.ds(0, clips - 1)]
-        unit_copy(unit, 3, most, most, partner).wait()
+        unit_copy(unit, 3, most, most, partner).wait_recv()
         return fin_refs[unit]
+
+    def sent(unit):
+        pair, got = pair_refs[unit], got_refs[unit]
+        unit_copy(unit, 0, pair, pair, partner).wait_send()
+        if NEAR[unit]:
+            near_copy(unit).wait_send()
+        for count in (got.shape[0] - 1, clips - 1):
+            most = got.at[pl.ds(0, count)]
+            unit_copy(unit, 2, most, most, partner).wait_send()
 
     big = rows // 2
 
@@ -473,14 +530,14 @@
     send_sums(st1, 1, *sums)
     for d in range(2, depth):
         along_x(1, d)
-        to_core(1, d)
+        along_y(d)
     along_z(2)
     along_x(2, 0)
     for d in range(depth):
-        to_core_late(1, d)
+        along_y_late(d)
+    y_to_core()
     most = par.at[pl.ds(0, frames - 1)]
     pltpu.make_async_copy(most, most, st_recv.at[0]).wait()
-    pltpu.make_async_copy(most, most, st_send.at[0]).wait()
     part_n = g1_ref.shape[0]
     part_w = g3_ref.shape[0]
     acc_n = [jnp.zeros((8, LANES), F32) for _ in range(nar_tiles)]
@@ -704,12 +761,12 @@
     send_sums(st6, 6, *sums)
     if own_gather:
         near(2)
-        far(5)
     grad_spatial(1)
     grad_spatial(2)
     if own_gather:
         near(3)
         near(4)
+        far(5)
 
     shift1, slope_gain1 = get_sums(st6, 6)
     along1, flat1 = back_terms(scale1, inv1, mean1, shift1, slope_gain1, inv_n)
@@ -785,22 +842,27 @@
         ge_out[...] = ge_ref[...]
     for index in range(3):
         weight_sent(index)
+    if own_gather:
+        for unit in range(units):
+            sent(unit)
+    for buf in (counts, st1, st2, st3, st4, st5, st6):
+        most = buf.at[pl.ds(0, devices - 1)]
+        pltpu.make_async_copy(most, most, st_send.at[0]).wait()
+    most = par.at[pl.ds(0, frames - 1)]
+    pltpu.make_async_copy(most, most, st_send.at[1]).wait()
     from_rows(gin_ref, 1).wait()
 
 
 def deliver_kernel(count, *refs):
     sources, targets, sems = refs[:count], refs[count : 2 * count], refs[2 * count]
-    copies = []
     for i in range(2):
         for j in range(sources[i].shape[0]):
             part = targets[i].at[:, :, LANES * j : LANES * (j + 1)]
-            copies.append(pltpu.make_async_copy(sources[i].at[j], part, sems.at[len(copies)]))
+            pltpu.make_async_copy(sources[i].at[j], part, sems.at[i]).start()
     for i in range(2, count):
-        copies.append(pltpu.make_async_copy(sources[i], targets[i], sems.at[len(copies)]))
-    for copy in copies:
-        copy.start()
-    for copy in copies:
-        copy.wait()
+        pltpu.make_async_copy(sources[i], targets[i], sems.at[i]).start()
+    for i in range(count):
+        pltpu.make_async_copy(sources[i], sources[i], sems.at[i]).wait()
 
 
 def deliver(arrays, big):
@@ -811,7 +873,7 @@
         out_shape=tuple(shapes),
         in_specs=[pl.BlockSpec(memory_space=pltpu.VMEM)] * count,
         out_specs=(pl.BlockSpec(memory_space=pl.ANY),) * count,
-        scratch_shapes=[pltpu.SemaphoreType.DMA((2 * arrays[0].shape[0] + count,))],
+        scratch_shapes=[pltpu.SemaphoreType.DMA((count,))],
         compiler_params=pltpu.CompilerParams(vmem_limit_bytes=1024 * 1024),
     )(*arrays)
 
@@ -839,7 +901,7 @@
     rows = pixels * slots
     tiles = channels // LANES
     devices = clips * frames
-    own_gather = all(n % 32 == 0 for n in (w_reduce.shape[0], w_spatial.shape[2], w_expand.shape[0]))
+    own_gather = clips == 4 and all(n % 32 == 0 for n in (w_reduce.shape[0], w_spatial.shape[2], w_expand.shape[0]))
     w_spatial = w_spatial.reshape(9, -1, narrow)
     if not own_gather:
         w_reduce = lax.all_gather(w_reduce, "frame", axis=0, tiled=True)
@@ -881,10 +943,13 @@
         cuts = [(height // frames // 2, width) for height, width in wholes]
         unit_scratch += [pltpu.VMEM((frames, half, width), BF16) for half, width in cuts]
         unit_scratch += [
-            pltpu.VMEM((frames // 2, half, width) if x_first else (frames, half, width // lines), BF16)
-            for (half, width), x_first in zip(cuts, X_FIRST)
+            pltpu.VMEM((frames // 2, half, width) if hop == "x" else (frames, half, width // lines), BF16)
+            for (half, width), hop in zip(cuts, NEAR)
         ]
-        unit_scratch += [pltpu.VMEM((frames, half, width // lines), BF16) for half, width in cuts]
+        unit_scratch += [
+            pltpu.VMEM((frames if hop else frames * lines, half, width // lines), BF16)
+            for (half, width), hop in zip(cuts, NEAR)
+        ]
         unit_scratch += [pltpu.VMEM((2 * half, width), BF16) for half, width in cuts]
 
     results = pl.pallas_call(
@@ -938,13 +1003,13 @@
             stats(2 * narrow // LANES),
             stats(2 * narrow // LANES),
             pltpu.SemaphoreType.DMA((5,)),
-            pltpu.SemaphoreType.DMA((3, 4, frames // 2)),
-            pltpu.SemaphoreType.DMA((3, 4, frames // 2)),
-            pltpu.SemaphoreType.DMA((8,)),
+            pltpu.SemaphoreType.DMA((3,)),
+            pltpu.SemaphoreType.DMA((3, frames + 3)),
+            pltpu.SemaphoreType.DMA((2,)),
             pltpu.SemaphoreType.DMA((8,)),
             pltpu.SemaphoreType.DMA((2,)),
-            pltpu.SemaphoreType.DMA((len(X_FIRST), 4)),
-            pltpu.SemaphoreType.DMA((len(X_FIRST), 4)),
+            pltpu.SemaphoreType.DMA((len(NEAR),)),
+            pltpu.SemaphoreType.DMA((len(NEAR), 4)),
             *unit_scratch,
         ],
         compiler_params=pltpu.CompilerParams(

time: 83.6 us -> 79.5 us (0.951)
  Pallas kernels: 82.1 us -> 78 us
    pallas_call x1, Pallas kernels: 80 us -> 76 us  [on_device(): pl.pallas_call(functools.partial(block_kernel, (clips, frames, side, own_...]
where the time goes in v4:
time: 79.5 us; the launch traced here: 79.3 us
  Pallas kernels  78 us (98%)
  between operations  1.3 us (2%)
    pallas_call x1, Pallas kernels, on_device(): pl.pallas_call(functools.partial(block_kernel, (clips, frames, side, own_...  76 us
    pallas_call x1, Pallas kernels, deliver(): pl.pallas_call(functools.partial(deliver_kernel, count), out_shape=tuple(...  1.99 us

profile of v4, /device:TPU:0, one launch (start us, length us, event | category | flops | bytes accessed | tf_op | source)
XLA Modules:
  0.0 79.3 jit_solution(2809540032669372909)
XLA Ops:
  1.3 76.0 %shard_map.212 = (bf16[8,400,2,128]{3,2,1,0:T(2,128)(2,1)S(1)}, bf16[8,400,2,128]{3,2,1,0:T(2,128)(2,1)S(1)}, f32[128,256]{1,0:T(8,128)S(1)}, f32[9,32,256]{2,1,...) custom-call(bf16[400,2,1024]{2,1,0:T(2,128)(2,1)} %bitcast.14, ...), custom_call_target="tpu_custom_call" | custom-call | tf_op jit(solution)/shard_map/pallas_call | solution.py:955
  77.3 2.0 %shard_map.213 = (bf16[400,2,1024]{2,1,0:T(2,128)(2,1)}, bf16[400,2,1024]{2,1,0:T(2,128)(2,1)}, f32[128,256]{1,0:T(8,128)}, f32[9,32,256]{2,1,0:T(8,128)}, f32[3...) custom-call(bf16[8,400,2,128]{3,2,1,0:T(2,128)(2,1)S(1)} %get-tuple-, ...), custom_call_target="tpu_custom_call" | custom-call | tf_op jit(solution)/shard_map/pallas_call | solution.py:871

commit v5 on v4

--- a/solution.py
+++ b/solution.py
@@ -259,6 +259,7 @@
     along = lax.div(frame, 2)
     depth = frames // 2
     x_peer = (clip, along * 2 + 1 - across)
+    xy_peer = (lax.rem(clip + 2, clips), along * 2 + 1 - across)
 
     def owner_at(d, side_x):
         return lax.rem(along - d + depth, depth) * 2 + side_x
@@ -315,15 +316,15 @@
         def along_y(d):
             weight_copy(1, 2 * depth + 1, owner_at(d, across), y_peer, own_columns(1)).start()
 
-        def along_y_late(d):
-            owner = owner_at(d, 1 - across)
-            weight_copy(1, depth + d, owner, partner, own_columns(1)).wait_recv()
-            weight_copy(1, 2 * depth + 2, owner, y_peer, own_columns(1)).start()
+        def along_xy(d):
+            weight_copy(1, 2 * depth + 2, owner_at(d, across), xy_peer, own_columns(1)).start()
 
         def y_to_core():
             blocks_wait(wrecv.at[1, 2 * depth + 1], blocks_of(1, depth - 1, False))
             for d in range(1, depth):
                 to_core(1, d)
+            for d in range(depth):
+                weight_copy(1, depth + d, owner_at(d, 1 - across), partner, own_columns(1)).wait_recv()
             blocks_wait(wrecv.at[1, 2 * depth + 2], blocks_of(1, depth, False))
             for d in range(depth):
                 weight_copy(1, 2 * depth, owner_at(d, 1 - across), partner).start()
@@ -347,7 +348,7 @@
         def nothing(*args):
             pass
 
-        along_z = along_x = along_y = along_y_late = y_to_core = nothing
+        along_z = along_x = along_y = along_xy = y_to_core = nothing
         to_core = to_core_late = weight_ready = weight_sent = nothing
 
     def send_params():
@@ -368,15 +369,22 @@
     along_x(0, 0)
     along_z(1)
     along_x(1, 0)
+    along_xy(0)
     gather_to_all(counts, 7)
     send_params()
     for d in range(1, depth):
         along_x(0, d)
         to_core(0, d)
     along_x(1, 1)
+    along_xy(1)
     along_y(1)
     for d in range(depth):
         to_core_late(0, d)
+
+    for d in range(2, depth):
+        along_x(1, d)
+        along_xy(d)
+        along_y(d)
 
     weight_ready(0)
 
@@ -528,13 +536,8 @@
 
     sums = lax.fori_loop(0, 2, conv_one, (zero_n, zero_n))
     send_sums(st1, 1, *sums)
-    for d in range(2, depth):
-        along_x(1, d)
-        along_y(d)
     along_z(2)
     along_x(2, 0)
-    for d in range(depth):
-        along_y_late(d)
     y_to_core()
     most = par.at[pl.ds(0, frames - 1)]
     pltpu.make_async_copy(most, most, st_recv.at[0]).wait()
@@ -705,19 +708,20 @@
     along3, flat3 = back_terms(scale3, inv3, mean3, shift3, slope_gain3, inv_w)
 
     def back_three(i, carry):
-        at = block_at(i)
+        at = pl.ds(pl.multiple_of(i * big, big), big)
         m = mask[at, :]
+        tiles = []
         for j in range(wide_tiles):
             lanes = slice(LANES * j, LANES * (j + 1))
             g = gt[at, lanes] * scale3[:, lanes] - pre3[at, lanes] * along3[:, lanes] - m * flat3[:, lanes]
-            gp3[at, lanes] = g.astype(BF16)
-        return carry
-
-    lax.fori_loop(0, blocks, back_three, 0)
-
-    d = dot(gp3[...], wet[...]) * slope2[...]
-    dz[...] = d
-    send_sums(st5, 5, part_sum(d), part_sum(d * ((pre2[...] - mean2) * inv2)))
+            tiles.append(g.astype(BF16))
+            gp3[at, lanes] = tiles[-1]
+        d = dot(jnp.concatenate(tiles, axis=1), wet[...]) * slope2[at, :]
+        dz[at, :] = d
+        return carry[0] + part_sum(d), carry[1] + part_sum(d * ((pre2[at, :] - mean2) * inv2))
+
+    sums = lax.fori_loop(0, 2, back_three, (zero_n, zero_n))
+    send_sums(st5, 5, *sums)
 
     def grad_expand(i, carry):
         lanes = pl.ds(pl.multiple_of(i * 256, 256), 256)

time: 79.5 us -> 77 us (0.969)
  Pallas kernels: 78 us -> 75.5 us
    pallas_call x1, Pallas kernels: 76 us -> 73.5 us  [on_device(): pl.pallas_call(functools.partial(block_kernel, (clips, frames, side, own_...]
where the time goes in v5:
time: 77 us; the launch traced here: 76.8 us
  Pallas kernels  75.5 us (98%)
  between operations  1.3 us (2%)
    pallas_call x1, Pallas kernels, on_device(): pl.pallas_call(functools.partial(block_kernel, (clips, frames, side, own_...  73.5 us
    pallas_call x1, Pallas kernels, deliver(): pl.pallas_call(functools.partial(deliver_kernel, count), out_shape=tuple(...  1.99 us

profile of v5, /device:TPU:0, one launch (start us, length us, event | category | flops | bytes accessed | tf_op | source)
XLA Modules:
  0.0 76.8 jit_solution(411198713727556661)
XLA Ops:
  1.3 73.5 %shard_map.212 = (bf16[8,400,2,128]{3,2,1,0:T(2,128)(2,1)S(1)}, bf16[8,400,2,128]{3,2,1,0:T(2,128)(2,1)S(1)}, f32[128,256]{1,0:T(8,128)S(1)}, f32[9,32,256]{2,1,...) custom-call(bf16[400,2,1024]{2,1,0:T(2,128)(2,1)} %bitcast.14, ...), custom_call_target="tpu_custom_call" | custom-call | tf_op jit(solution)/shard_map/pallas_call | solution.py:959
  74.8 2.0 %shard_map.213 = (bf16[400,2,1024]{2,1,0:T(2,128)(2,1)}, bf16[400,2,1024]{2,1,0:T(2,128)(2,1)}, f32[128,256]{1,0:T(8,128)}, f32[9,32,256]{2,1,0:T(8,128)}, f32[3...) custom-call(bf16[8,400,2,128]{3,2,1,0:T(2,128)(2,1)S(1)} %get-tuple-, ...), custom_call_target="tpu_custom_call" | custom-call | tf_op jit(solution)/shard_map/pallas_call | solution.py:875

commit v6 on v5

--- a/solution.py
+++ b/solution.py
@@ -86,7 +86,8 @@
     dz,
     spad,
     act2,
-    nine,
+    still,
+    moved,
     pre3,
     gt,
     gp3,
@@ -125,7 +126,8 @@
     wide_tiles = channels // LANES
     nar_tiles = narrow // LANES
     blocks = rows // BLOCK
-    pad = 2 * side
+    step_rows = 2 * side
+    pad = step_rows + 8
     lines = clips // 2
     line_me = lax.div(clip, 2)
     y_peer = (lax.rem(clip + 2, clips), frame)
@@ -197,8 +199,10 @@
     bound = jnp.where(slot == 0, limit[0], limit[1])
     live = ((line < bound) & (col < bound)).astype(F32)
     mask[...] = live
-    left_ok[...] = (col >= 1).astype(F32)
-    right_ok[...] = (col <= side - 2).astype(F32)
+    for ref, ok in ((left_ok, col >= 1), (right_ok, col <= side - 2)):
+        ref[0:8, :] = jnp.zeros((8, LANES), F32)
+        ref[8 : 8 + rows, :] = ok.astype(F32)
+        ref[8 + rows : 16 + rows, :] = jnp.zeros((8, LANES), F32)
 
     par[frame] = jnp.zeros((8, LANES), F32)
     for i, ref in enumerate((g1_ref, b1_ref, g2_ref, b2_ref, g3_ref, b3_ref)):
@@ -221,9 +225,12 @@
         return carry
 
     lax.fori_loop(0, blocks, mask_in, 0)
-    edge = jnp.zeros((3, pad, narrow), F32)
-    spad[:, 0:pad, :] = edge
-    spad[:, pad + rows : 2 * pad + rows, :] = edge
+    edge = jnp.zeros((pad, narrow), F32)
+    spad[0:pad, :] = edge
+    spad[pad + rows : 2 * pad + rows, :] = edge
+    edge = jnp.zeros((3, step_rows - 8, narrow), BF16)
+    moved[:, 0 : step_rows - 8, :] = edge
+    moved[:, step_rows + 8 + rows : 2 * step_rows + rows, :] = edge
     turned = xm[...].T
     if own_gather:
         piece = part_r // 2
@@ -450,53 +457,44 @@
             return carry
 
         lax.fori_loop(0, frames, add, 0)
-        if NEAR[unit]:
-            near_copy(unit).start()
+        near_copy(unit).start()
 
     def far(unit):
         pair, mid, got = pair_refs[unit], mid_refs[unit], got_refs[unit]
         cut = pair.shape[2] // lines
-        if NEAR[unit]:
-            near_copy(unit).wait_recv()
+        near_copy(unit).wait_recv()
 
         def add(k, carry):
             own = pair[2 * k + across] if NEAR[unit] == "x" else pair[k, :, columns(line_me, cut)]
             mid[k] = (mid[k].astype(F32) + own.astype(F32)).astype(BF16)
             return carry
 
-        if NEAR[unit]:
-            lax.fori_loop(0, mid.shape[0], add, 0)
-        if not NEAR[unit]:
-            slot_me = line_me * frames + frame
-            got[slot_me] = pair[frame, :, columns(line_me, cut)]
-
-            def send(k, carry):
-                line = lax.rem(line_me + lax.div(k, frames), lines)
-                owner = lax.rem(frame + lax.rem(k, frames), frames)
-                src = pair.at[owner, :, columns(line, cut)]
-                unit_copy(unit, 2, src, got.at[slot_me], (line * 2 + core, owner)).start()
-                return carry
-
-        elif NEAR[unit] == "x":
+        lax.fori_loop(0, mid.shape[0], add, 0)
+        if NEAR[unit] == "x":
             slot_me = line_me * depth + along
             got[slot_me] = mid[along, :, columns(line_me, cut)]
 
             def send(k, carry):
-                line = lax.rem(line_me + lax.div(k, depth), lines)
-                deep = lax.rem(along + lax.rem(k, depth), depth)
-                src = mid.at[deep, :, columns(line, cut)]
-                unit_copy(unit, 2, src, got.at[slot_me], (line * 2 + core, deep * 2 + across)).start()
+                deep, line = lax.div(k, lines), lax.rem(k, lines)
+
+                @pl.when(jnp.logical_or(deep != along, line != line_me))
+                def _():
+                    src = mid.at[deep, :, columns(line, cut)]
+                    unit_copy(unit, 2, src, got.at[slot_me], (line * 2 + core, deep * 2 + across)).start()
+
                 return carry
 
         else:
             got[frame] = mid[frame]
 
-            def send(k, carry):
-                owner = lax.rem(frame + k, frames)
-                unit_copy(unit, 2, mid.at[owner], got.at[frame], (clip, owner)).start()
+            def send(owner, carry):
+                @pl.when(owner != frame)
+                def _():
+                    unit_copy(unit, 2, mid.at[owner], got.at[frame], (clip, owner)).start()
+
                 return carry
 
-        lax.fori_loop(1, got.shape[0], send, 0)
+        lax.fori_loop(0, got.shape[0], send, 0)
 
     def owners(unit):
         got, fin = got_refs[unit], fin_refs[unit]
@@ -520,8 +518,7 @@
     def sent(unit):
         pair, got = pair_refs[unit], got_refs[unit]
         unit_copy(unit, 0, pair, pair, partner).wait_send()
-        if NEAR[unit]:
-            near_copy(unit).wait_send()
+        near_copy(unit).wait_send()
         for count in (got.shape[0] - 1, clips - 1):
             most = got.at[pl.ds(0, count)]
             unit_copy(unit, 2, most, most, partner).wait_send()
@@ -572,7 +569,7 @@
         s = sigmoid(z)
         m = both(mask[at, :])
         ms = m * s
-        spad[1, pl.ds(pl.multiple_of(i * BLOCK + pad, 8), BLOCK), :] = ms * z
+        spad[pl.ds(pl.multiple_of(i * BLOCK + pad, 16), BLOCK), :] = ms * z
         slope1[at, :] = ms * (1.0 + z * (1.0 - s))
         return carry
 
@@ -581,27 +578,34 @@
     def spread():
         def shifted(i, carry):
             at = block_at(i)
-            v = spad[1, pl.ds(pl.multiple_of(i * BLOCK + pad - 8, 8), BLOCK + 16), :]
-            here = pl.ds(pl.multiple_of(i * BLOCK + pad, 8), BLOCK)
-            spad[0, here, :] = pltpu.roll(v, 2, 0)[8 : 8 + BLOCK] * both(left_ok[at, :])
-            spad[2, here, :] = pltpu.roll(v, BLOCK + 14, 0)[8 : 8 + BLOCK] * both(right_ok[at, :])
+            v = spad[pl.ds(pl.multiple_of(i * BLOCK + pad - 8, 8), BLOCK + 24), :]
+            span = pl.ds(pl.multiple_of(i * BLOCK + 8, 8), BLOCK + 8)
+            three = (
+                pltpu.roll(v, 2, 0)[8 : 16 + BLOCK] * both(left_ok[span, :]),
+                v[8 : 16 + BLOCK],
+                pltpu.roll(v, BLOCK + 22, 0)[8 : 16 + BLOCK] * both(right_ok[span, :]),
+            )
+            there = pl.ds(pl.multiple_of(i * BLOCK + pad, 16), BLOCK)
+            for j in range(3):
+                still[j, at, :] = three[j][0:BLOCK].astype(BF16)
+                moved[j, there, :] = three[j][8 : 8 + BLOCK].astype(BF16)
             return carry
 
         lax.fori_loop(0, blocks, shifted, 0)
-
-    def gather_nine(flip):
-        def step(i, carry):
-            at = block_at(i)
-            for tap in range(9):
-                row_off, col_off = (tap // 3, tap % 3) if not flip else (2 - tap // 3, 2 - tap % 3)
-                src = pl.ds(pl.multiple_of(i * BLOCK + pad * row_off, 8), BLOCK)
-                nine[at, narrow * tap : narrow * (tap + 1)] = spad[col_off, src, :].astype(BF16)
-            return carry
-
-        lax.fori_loop(0, blocks, step, 0)
+        for j in range(3):
+            head = jnp.concatenate([jnp.zeros((8, narrow), F32), still[j, 0:16, :].astype(F32)[0:8]], axis=0)
+            moved[j, pad - 16 : pad, :] = head.astype(BF16)
+
+    def taps(start, count, chosen, flip):
+        parts = []
+        for tap in chosen:
+            row_off, col_off = (tap // 3, tap % 3) if not flip else (2 - tap // 3, 2 - tap % 3)
+            ref = still if row_off == 1 else moved
+            first = start if row_off < 2 else start + 2 * step_rows
+            parts.append(ref[col_off, pl.ds(pl.multiple_of(first, 16), count), :])
+        return jnp.concatenate(parts, axis=1)
 
     spread()
-    gather_nine(False)
     weight_ready(1)
     for d in range(1, depth):
         along_x(2, d)
@@ -609,7 +613,7 @@
 
     def conv_two(i, carry):
         at = pl.ds(pl.multiple_of(i * big, big), big)
-        v = dot(nine[at, :], ws[...].reshape(9 * narrow, narrow))
+        v = dot(taps(i * big, big, range(9), False), ws[...].reshape(9 * narrow, narrow))
         pre2[at, :] = v
         mv = both(mask[at, :]) * v
         return carry[0] + part_sum(mv), carry[1] + part_sum(mv * v)
@@ -617,7 +621,7 @@
     sums = lax.fori_loop(0, 2, conv_two, (zero_n, zero_n))
     send_sums(st2, 2, *sums)
     wrt[...] = wr[...].T
-    a1t[...] = spad[1, pad : pad + rows, :].astype(BF16).T
+    a1t[...] = still[1].T
     for d in range(depth):
         to_core_late(2, d)
 
@@ -738,18 +742,16 @@
 
     def back_two(i, carry):
         at = block_at(i)
-        here = pl.ds(pl.multiple_of(i * BLOCK + pad, 8), BLOCK)
+        here = pl.ds(pl.multiple_of(i * BLOCK + pad, 16), BLOCK)
         m = both(mask[at, :])
-        spad[1, here, :] = dz[at, :] * scale2 - m * (pre2[at, :] * along2 + flat2)
+        spad[here, :] = dz[at, :] * scale2 - m * (pre2[at, :] * along2 + flat2)
         return carry
 
     lax.fori_loop(0, blocks, back_two, 0)
     spread()
-    gather_nine(True)
 
     def grad_spatial(row):
-        wide_row = 3 * narrow
-        gs_refs[row][...] = dot(a1t[...], nine[:, wide_row * row : wide_row * (row + 1)]).astype(BF16)
+        gs_refs[row][...] = dot(a1t[...], taps(0, rows, range(3 * row, 3 * row + 3), True)).astype(BF16)
         if own_gather:
             cores(2 + row).start()
 
@@ -757,7 +759,7 @@
 
     def back_spatial(i, carry):
         at = pl.ds(pl.multiple_of(i * big, big), big)
-        d = dot(nine[at, :], wst[...]) * slope1[at, :]
+        d = dot(taps(i * big, big, range(9), True), wst[...]) * slope1[at, :]
         dz[at, :] = d
         return carry[0] + part_sum(d), carry[1] + part_sum(d * ((pre1[at, :] - mean1) * inv1))
 
@@ -924,6 +926,7 @@
     narrow_f32 = pltpu.VMEM((rows, narrow), F32)
     wide_f32 = pltpu.VMEM((rows, channels), F32)
     lanes_f32 = pltpu.VMEM((rows, LANES), F32)
+    edges_f32 = pltpu.VMEM((rows + 16, LANES), F32)
 
     def stats(count):
         return pltpu.VMEM((devices, count, LANES), F32)
@@ -978,8 +981,8 @@
             pltpu.VMEM((narrow, rows), BF16),
             pltpu.VMEM((narrow, rows), BF16),
             lanes_f32,
-            lanes_f32,
-            lanes_f32,
+            edges_f32,
+            edges_f32,
             pltpu.VMEM((channels, narrow), BF16),
             pltpu.VMEM((9, narrow, narrow), BF16),
             pltpu.VMEM((narrow, channels), BF16),
@@ -991,9 +994,10 @@
             narrow_f32,
             narrow_f32,
             narrow_f32,
-            pltpu.VMEM((3, rows + 4 * side, narrow), F32),
+            pltpu.VMEM((rows + 4 * side + 16, narrow), F32),
             pltpu.VMEM((rows, narrow), BF16),
-            pltpu.VMEM((rows, 9 * narrow), BF16),
+            pltpu.VMEM((3, rows, narrow), BF16),
+            pltpu.VMEM((3, rows + 4 * side, narrow), BF16),
             wide_f32,
             wide_f32,
             pltpu.VMEM((rows, channels), BF16),

time: 77 us -> 76.7 us (level)
  no operation moved by 1% of the time
where the time goes in v6:
time: 76.7 us; the launch traced here: 76.6 us
  Pallas kernels  75.3 us (98%)
  between operations  1.3 us (2%)
    pallas_call x1, Pallas kernels, on_device(): pl.pallas_call(functools.partial(block_kernel, (clips, frames, side, own_...  73.3 us
    pallas_call x1, Pallas kernels, deliver(): pl.pallas_call(functools.partial(deliver_kernel, count), out_shape=tuple(...  1.99 us

profile of v6, /device:TPU:0, one launch (start us, length us, event | category | flops | bytes accessed | tf_op | source)
XLA Modules:
  0.0 76.6 jit_solution(18087471652720461215)
XLA Ops:
  1.3 73.3 %shard_map.212 = (bf16[8,400,2,128]{3,2,1,0:T(2,128)(2,1)S(1)}, bf16[8,400,2,128]{3,2,1,0:T(2,128)(2,1)S(1)}, f32[128,256]{1,0:T(8,128)S(1)}, f32[9,32,256]{2,1,...) custom-call(bf16[400,2,1024]{2,1,0:T(2,128)(2,1)} %bitcast.14, ...), custom_call_target="tpu_custom_call" | custom-call | tf_op jit(solution)/shard_map/pallas_call | solution.py:962
  74.6 2.0 %shard_map.213 = (bf16[400,2,1024]{2,1,0:T(2,128)(2,1)}, bf16[400,2,1024]{2,1,0:T(2,128)(2,1)}, f32[128,256]{1,0:T(8,128)}, f32[9,32,256]{2,1,0:T(8,128)}, f32[3...) custom-call(bf16[8,400,2,128]{3,2,1,0:T(2,128)(2,1)S(1)} %get-tuple-, ...), custom_call_target="tpu_custom_call" | custom-call | tf_op jit(solution)/shard_map/pallas_call | solution.py:877

commit v7 on v6

--- a/solution.py
+++ b/solution.py
@@ -294,7 +294,7 @@
                 src_ref=part,
                 dst_ref=part,
                 send_sem=wsend.at[index],
-                recv_sem=wrecv.at[index, sem],
+                recv_sem=wrecv.at[weight_sems[index][sem]],
                 device_id=target,
                 device_id_type=MESH,
             )
@@ -309,6 +309,15 @@
         def blocks_wait(sem, view):
             pltpu.make_async_copy(view, view, sem).wait()
 
+        numbers = iter(range(wrecv.shape[0]))
+        weight_sems = []
+        for index in range(3):
+            own = {d: next(numbers) for d in range(1, depth)}
+            together = next(numbers) if index == 1 else None
+            own |= {depth + d: next(numbers) if together is None else together for d in range(depth)}
+            own |= {2 * depth + k: next(numbers) for k in range(3 if index == 1 else 1)}
+            weight_sems.append(own)
+
         def along_z(index):
             for d in range(1, depth):
                 target = (clip, lax.rem(along + d, depth) * 2 + across)
@@ -327,12 +336,11 @@
             weight_copy(1, 2 * depth + 2, owner_at(d, across), xy_peer, own_columns(1)).start()
 
         def y_to_core():
-            blocks_wait(wrecv.at[1, 2 * depth + 1], blocks_of(1, depth - 1, False))
+            blocks_wait(wrecv.at[weight_sems[1][2 * depth + 1]], blocks_of(1, depth - 1, False))
             for d in range(1, depth):
                 to_core(1, d)
-            for d in range(depth):
-                weight_copy(1, depth + d, owner_at(d, 1 - across), partner, own_columns(1)).wait_recv()
-            blocks_wait(wrecv.at[1, 2 * depth + 2], blocks_of(1, depth, False))
+            blocks_wait(wrecv.at[weight_sems[1][depth]], blocks_of(1, depth, False))
+            blocks_wait(wrecv.at[weight_sems[1][2 * depth + 2]], blocks_of(1, depth, False))
             for d in range(depth):
                 weight_copy(1, 2 * depth, owner_at(d, 1 - across), partner).start()
 
@@ -345,7 +353,7 @@
             weight_copy(index, 2 * depth, owner, partner).start()
 
         def weight_ready(index):
-            blocks_wait(wrecv.at[index, 2 * depth], blocks_of(index, 2 * depth - 1))
+            blocks_wait(wrecv.at[weight_sems[index][2 * depth]], blocks_of(index, 2 * depth - 1))
 
         def weight_sent(index):
             blocks_wait(wsend.at[index], blocks_of(index, 4 * depth - 2))
@@ -384,13 +392,13 @@
         to_core(0, d)
     along_x(1, 1)
     along_xy(1)
-    along_y(1)
     for d in range(depth):
         to_core_late(0, d)
 
     for d in range(2, depth):
         along_x(1, d)
         along_xy(d)
+    for d in range(1, depth):
         along_y(d)
 
     weight_ready(0)
@@ -1012,7 +1020,7 @@
             stats(2 * narrow // LANES),
             pltpu.SemaphoreType.DMA((5,)),
             pltpu.SemaphoreType.DMA((3,)),
-            pltpu.SemaphoreType.DMA((3, frames + 3)),
+            pltpu.SemaphoreType.DMA((3 * frames,)),
             pltpu.SemaphoreType.DMA((2,)),
             pltpu.SemaphoreType.DMA((8,)),
             pltpu.SemaphoreType.DMA((2,)),

time: 76.7 us -> 76.7 us (level)
  no operation moved by 1% of the time
where the time goes in v7:
time: 76.7 us; the launch traced here: 76.5 us
  Pallas kernels  75.2 us (98%)
  between operations  1.3 us (2%)
    pallas_call x1, Pallas kernels, on_device(): pl.pallas_call(functools.partial(block_kernel, (clips, frames, side, own_...  73.2 us
    pallas_call x1, Pallas kernels, deliver(): pl.pallas_call(functools.partial(deliver_kernel, count), out_shape=tuple(...  1.99 us

profile of v7, /device:TPU:0, one launch (start us, length us, event | category | flops | bytes accessed | tf_op | source)
XLA Modules:
  0.0 76.5 jit_solution(5174031865145492439)
XLA Ops:
  1.3 73.2 %shard_map.212 = (bf16[8,400,2,128]{3,2,1,0:T(2,128)(2,1)S(1)}, bf16[8,400,2,128]{3,2,1,0:T(2,128)(2,1)S(1)}, f32[128,256]{1,0:T(8,128)S(1)}, f32[9,32,256]{2,1,...) custom-call(bf16[400,2,1024]{2,1,0:T(2,128)(2,1)} %bitcast.14, ...), custom_call_target="tpu_custom_call" | custom-call | tf_op jit(solution)/shard_map/pallas_call | solution.py:970
  74.5 2.0 %shard_map.213 = (bf16[400,2,1024]{2,1,0:T(2,128)(2,1)}, bf16[400,2,1024]{2,1,0:T(2,128)(2,1)}, f32[128,256]{1,0:T(8,128)}, f32[9,32,256]{2,1,0:T(8,128)}, f32[3...) custom-call(bf16[8,400,2,128]{3,2,1,0:T(2,128)(2,1)S(1)} %get-tuple-, ...), custom_call_target="tpu_custom_call" | custom-call | tf_op jit(solution)/shard_map/pallas_call | solution.py:885

commit v8 on v7

--- a/solution.py
+++ b/solution.py
@@ -13,7 +13,7 @@
 BLOCK = 80
 VMEM_BYTES = 52 * 1024 * 1024
 MESH = pl.DeviceIdType.MESH
-NEAR = ("x", "y", "y", "x", "y", "x")
+NEAR = ("x", "y", "x", "y", "x", "y")
 F32 = jnp.float32
 BF16 = jnp.bfloat16
 

time: 76.7 us -> 76.6 us (level)
  no operation moved by 1% of the time
where the time goes in v8:
time: 76.6 us; the launch traced here: 76.5 us
  Pallas kernels  75.2 us (98%)
  between operations  1.3 us (2%)
    pallas_call x1, Pallas kernels, on_device(): pl.pallas_call(functools.partial(block_kernel, (clips, frames, side, own_...  73.2 us
    pallas_call x1, Pallas kernels, deliver(): pl.pallas_call(functools.partial(deliver_kernel, count), out_shape=tuple(...  1.99 us

profile of v8, /device:TPU:0, one launch (start us, length us, event | category | flops | bytes accessed | tf_op | source)
XLA Modules:
  0.0 76.5 jit_solution(8145764825129487235)
XLA Ops:
  1.3 73.2 %shard_map.212 = (bf16[8,400,2,128]{3,2,1,0:T(2,128)(2,1)S(1)}, bf16[8,400,2,128]{3,2,1,0:T(2,128)(2,1)S(1)}, f32[128,256]{1,0:T(8,128)S(1)}, f32[9,32,256]{2,1,...) custom-call(bf16[400,2,1024]{2,1,0:T(2,128)(2,1)} %bitcast.14, ...), custom_call_target="tpu_custom_call" | custom-call | tf_op jit(solution)/shard_map/pallas_call | solution.py:970
  74.5 2.0 %shard_map.213 = (bf16[400,2,1024]{2,1,0:T(2,128)(2,1)}, bf16[400,2,1024]{2,1,0:T(2,128)(2,1)}, f32[128,256]{1,0:T(8,128)}, f32[9,32,256]{2,1,0:T(8,128)}, f32[3...) custom-call(bf16[8,400,2,128]{3,2,1,0:T(2,128)(2,1)S(1)} %get-tuple-, ...), custom_call_target="tpu_custom_call" | custom-call | tf_op jit(solution)/shard_map/pallas_call | solution.py:885
